TPU v7x, 32 devices: a whole 2x2x4 slice. The times are simulated.
32 devices in a mesh: dp: 16 (over z, x, core), ctx: 2 (over y).
Axes of the slice: x: 2, y: 2, z: 4, core: 2. Of those that a mesh axis runs over, the one named last changes fastest.
Arguments:
- projections: bfloat16 [8192, 6144], P(('dp', 'ctx')), may hold values from -6 to 6
- block_source: int32 [16, 2, 2], P('dp', 'ctx'), may hold values from 0 to 63, as said below
- clip_ids: int32 [16, 4], P('dp'), may hold values from 0 to 2, as said below
- out_weight: bfloat16 [2048, 1536], P('dp'), may hold values from -1 to 1
Outputs:
- mixed: bfloat16 [8192, 1536], P(('dp', 'ctx'))
Inputs may be any that keep to these rules, and one draw needn't show every extreme that they name: `block_source`: arrival block a lies on the device numbered a // 2 in dp-major order (dp index a // (2 * 2), ctx index (a // 2) % 2). The block that fills pack block (o, j, l) lies on the device with the same ctx index j and dp index o or o XOR 1. Every arrival block fills exactly one pack block. `clip_ids`: in each pack the clip numbers start at 0, never fall and rise by at most one from block to block; every clip spans 1 to 2 blocks, and in every pack some clip spans exactly 2 blocks.
All inputs are finite; a program needn't handle non-finite values.
Results may differ from a plain program's by a relative error of at most 0.0057.
Values may be sent and summed in bfloat16 or wider, within the bound.
No kernel may reach another device: no remote copies, remote signals or barrier semaphores. Data moves between devices by JAX's collectives and lax.ppermute only.
A program may use at most 64 MiB of HBM per device.

v0:
```python
import functools
import math

import jax
import jax.numpy as jnp
from jax import lax
from jax.experimental import pallas as pl
from jax.experimental.pallas import tpu as pltpu
from jax.sharding import PartitionSpec as P

HEAD = 128


big_negative = -1e30
MIB = 1 << 20


def partner(value, axis, bit):
    mask = 2**bit
    pairs = [(source, source ^ mask) for source in range(lax.axis_size(axis))]
    return lax.ppermute(value, axis, pairs)


def soft_weights(scores, allowed):
    masked = jnp.where(allowed, scores, big_negative)
    row_max = jnp.max(masked, axis=-1, keepdims=True)
    exponent = jnp.exp(masked - row_max)
    return (exponent / jnp.sum(exponent, axis=-1, keepdims=True)).astype(jnp.bfloat16)


def attend_dense(queries, key_rows, value_rows, token_clip, scaling):
    token_count, head_count, head_size = queries.shape
    step_size = min(token_count, 512)
    step_count = token_count // step_size
    query_steps = queries.reshape(step_count, step_size, head_count, head_size)
    clip_steps = token_clip.reshape(step_count, step_size)

    def one_step(arguments):
        query_block, clip_block = arguments
        scores = (
            jnp.einsum("qhe,khe->hqk", query_block, key_rows, preferred_element_type=jnp.float32)
            * scaling
        )
        allowed = (clip_block[:, None] == token_clip[None, :])[None]
        weights = soft_weights(scores, allowed)
        return jnp.einsum(
            "hqk,khe->qhe", weights, value_rows, preferred_element_type=jnp.float32
        ).astype(jnp.bfloat16)

    outputs = lax.map(one_step, (query_steps, clip_steps))
    return outputs.reshape(token_count, head_count, head_size)


def body_general(projections, block_source, clip_ids, out_weight):
    ctx_count = lax.axis_size("ctx")
    local_rows, row_width = projections.shape
    local_blocks = block_source.shape[2]
    block_rows = local_rows // local_blocks
    own_blocks = projections.reshape(local_blocks, block_rows, row_width)
    partner_blocks = partner(own_blocks, "dp", 0)
    source_ids = block_source.reshape(local_blocks)
    from_partner = source_ids // (local_blocks * ctx_count) != lax.axis_index("dp")
    chosen_slot = source_ids % local_blocks + local_blocks * from_partner.astype(jnp.int32)
    candidates = jnp.concatenate([own_blocks, partner_blocks], axis=0)
    packed = jnp.take(candidates, chosen_slot, axis=0)
    local_heads = row_width // (3 * HEAD) // ctx_count
    grouped = packed.reshape(local_rows, ctx_count, local_heads, 3 * HEAD)
    block_clip = clip_ids.reshape(-1)
    token_clip = jnp.repeat(block_clip, block_rows)
    scaling = 1.0 / math.sqrt(HEAD)
    regrouped = lax.all_to_all(grouped, "ctx", split_axis=1, concat_axis=0, tiled=True)
    token_count = regrouped.shape[0]
    item_count = regrouped.shape[2]
    features = regrouped.reshape(token_count, item_count, 3 * HEAD)
    queries = features[:, :, :HEAD]
    key_rows = features[:, :, HEAD : 2 * HEAD]
    value_rows = features[:, :, 2 * HEAD :]
    attended = attend_dense(queries, key_rows, value_rows, token_clip, scaling)
    merged = attended.reshape(local_rows * ctx_count, local_heads * HEAD)
    attention_rows = lax.all_to_all(merged, "ctx", split_axis=0, concat_axis=1, tiled=True)
    result = jnp.dot(
        attention_rows,
        lax.all_gather(out_weight, "dp", axis=0, tiled=True),
        preferred_element_type=jnp.float32,
    )
    return result.astype(jnp.bfloat16)


def stage_kernel(source_ref, own_ref, out_ref, sem):
    copy = pltpu.make_async_copy(own_ref, out_ref, sem)
    copy.start()
    copy.wait()


def pack_kernel(source_ref, own_ref, partner_ref, rows_ref, *rest):
    halo_refs, sems = rest[:-1], rest[-1]
    ctx, dp = lax.axis_index("ctx"), lax.axis_index("dp")
    slots = own_ref.shape[0]
    for which, block in ((1, 1 - ctx), (0, ctx)):
        source = source_ref[0, 0, block]
        slot = lax.rem(source, slots)
        away = source // (2 * slots) != dp

        @pl.when(jnp.logical_not(away))
        def _():
            pltpu.make_async_copy(own_ref.at[slot], rows_ref.at[which], sems.at[which]).start()

        @pl.when(away)
        def _():
            pltpu.make_async_copy(partner_ref.at[slot], rows_ref.at[which], sems.at[which]).start()

    pltpu.make_async_copy(own_ref.at[0], rows_ref.at[1], sems.at[1]).wait()
    first = HEAD
    for halo_ref in halo_refs:
        for at in range(0, halo_ref.shape[1], 2 * HEAD):
            halo_ref[:, at : at + 2 * HEAD] = rows_ref[1, :, first : first + 2 * HEAD]
            first += 3 * HEAD
    pltpu.make_async_copy(own_ref.at[0], rows_ref.at[0], sems.at[0]).wait()


def attend(heads, load_queries, load_own, load_more, allowed, out_ref, other_ref):
    scaling = math.log2(math.e) / math.sqrt(HEAD)
    contract_last = (((1,), (1,)), ((), ()))
    ones = jnp.ones((2 * out_ref.shape[0], HEAD), jnp.bfloat16)
    odd_core = lax.rem(lax.axis_index("dp"), 2) == 1
    for start in range(0, heads, 4):
        group = min(4, heads - start)
        scores = []
        for head in range(start, start + group):
            queries = load_queries(head)
            pair = []
            for loader in (load_own, load_more):
                pair.append(
                    lax.dot_general(
                        queries, loader(head, 0), contract_last, preferred_element_type=jnp.float32
                    )
                    * scaling
                )
            scores.append(pair)
        weights = []
        for own, more in scores:
            more = jnp.where(allowed, more, big_negative)
            row_max = jnp.max(jnp.maximum(own, more), axis=-1, keepdims=True)
            weights.append(
                jnp.concatenate(
                    [
                        jnp.exp2(own - row_max).astype(jnp.bfloat16),
                        jnp.exp2(more - row_max).astype(jnp.bfloat16),
                    ],
                    axis=1,
                )
            )
        outs = []
        for head in range(start, start + group):
            values = jnp.concatenate([load_own(head, 1), load_more(head, 1)], axis=0)
            sums = jnp.dot(
                weights[head - start],
                jnp.concatenate([values, ones], axis=1),
                preferred_element_type=jnp.float32,
            )
            outs.append(sums[:, :HEAD] / sums[:, HEAD:])
            out_ref[:, head * HEAD : (head + 1) * HEAD] = outs[-1].astype(jnp.bfloat16)
        for pair in range(group // 2):
            at = (start // 2 + pair) * HEAD
            other = jnp.where(odd_core, outs[2 * pair], outs[2 * pair + 1])
            other_ref[:, at : at + HEAD] = other.astype(jnp.bfloat16)


def inner_kernel(clip_ref, rows_ref, out_ref, other_ref):
    ctx = lax.axis_index("ctx")
    allowed = clip_ref[0, 2 * ctx] == clip_ref[0, 2 * ctx + 1]

    def loader(block):
        def get(head, which):
            first = (head * 3 + 1 + which) * HEAD
            return rows_ref[block, :, first : first + HEAD]

        return get

    attend(
        out_ref.shape[1] // HEAD,
        lambda head: loader(0)(head, -1),
        loader(0),
        loader(1),
        allowed,
        out_ref,
        other_ref,
    )


def edge_kernel(first_head, clip_ref, rows_ref, halo_ref, out_ref, other_ref):
    ctx = lax.axis_index("ctx")
    edge_clip = clip_ref[0, 1 + ctx]
    crosses = edge_clip == clip_ref[0, 2 - ctx]
    allowed = jnp.logical_or(crosses, edge_clip == clip_ref[0, 3 * ctx])

    def load_own(head, which):
        first = ((first_head + head) * 3 + 1 + which) * HEAD
        return rows_ref[1, :, first : first + HEAD]

    def load_more(head, which):
        first = ((first_head + head) * 3 + 1 + which) * HEAD
        at = (2 * head + which) * HEAD
        return jnp.where(crosses, halo_ref[:, at : at + HEAD], rows_ref[0, :, first : first + HEAD])

    attend(
        out_ref.shape[1] // HEAD,
        lambda head: load_own(head, -1),
        load_own,
        load_more,
        allowed,
        out_ref,
        other_ref,
    )


def ring_order(lines):
    return list(range(0, lines, 2)) + list(range(1, lines, 2))[::-1]


def shard_places(origins, depth):
    index = lax.axis_index("dp")
    core, side, line = lax.rem(index, 2), lax.rem(index // 2, 2), index // 4
    places = ring_order(lax.axis_size("dp") // 4)
    found = []
    for steps, other_side in origins:
        from_line = line
        for at, place in enumerate(places):
            from_line = jnp.where(line == place, places[at - steps], from_line)
        pair = from_line * 2 + (1 - side if other_side else side)
        here = pl.ds(pl.multiple_of((pair * 2 + core) * depth, depth), depth)
        there = pl.ds(pl.multiple_of(pair * depth, depth), depth)
        found.append((here, there))
    return found


def inner_project_kernel(origins, early, inner_ref, their_ref, *rest):
    shard_refs, (total_ref, left_ref, features) = rest[:-3], rest[-3:]
    block = inner_ref.shape[0]
    depth = left_ref.shape[1] // (len(origins) - early)
    for number, (here, there) in enumerate(shard_places(origins, depth)):
        ref, at = (features, number) if number < early else (left_ref, number - early)
        ref[:block, at * depth : (at + 1) * depth] = inner_ref[:, here]
        ref[block:, at * depth : (at + 1) * depth] = their_ref[:, there]
    tile = 2 * HEAD
    for first in range(0, total_ref.shape[1], tile):
        columns = slice(first, first + tile)
        weight = jnp.concatenate([ref[:, columns] for ref in shard_refs], axis=0)
        total_ref[:, columns] = jnp.dot(
            features[...], weight, preferred_element_type=jnp.float32
        )


def arrange_kernel(origins, parts, *refs):
    edge_refs, their_refs = refs[:parts], refs[parts : 2 * parts]
    out_ref, edge_rows, their_rows = refs[2 * parts :]
    for refs, held in ((edge_refs, edge_rows), (their_refs, their_rows)):
        first = 0
        for ref in refs:
            held[:, first : first + ref.shape[1]] = ref[...]
            first += ref.shape[1]
    block = edge_rows.shape[0]
    depth = out_ref.shape[1] // len(origins)
    for number, (here, there) in enumerate(shard_places(origins, depth)):
        at = slice(number * depth, (number + 1) * depth)
        out_ref[:block, at] = edge_rows[:, here]
        out_ref[block:, at] = their_rows[:, there]


def edge_project_kernel(edge_ref, left_ref, inner_total_ref, *rest):
    shard_refs, total_ref = rest[:-1], rest[-1]
    rows = edge_ref.shape[0]
    depths = sum(ref.shape[0] for ref in shard_refs)
    depth = edge_ref.shape[1] - depths
    left = left_ref.shape[1] - depth
    tile = 2 * HEAD
    for first in range(0, total_ref.shape[1], tile):
        columns = slice(first, first + tile)
        weight = jnp.concatenate([ref[:, columns] for ref in shard_refs], axis=0)
        total_ref[:rows, columns] = inner_total_ref[:, columns] + jnp.dot(
            left_ref[:, :left], weight[-left:], preferred_element_type=jnp.float32
        )
        total_ref[rows:, columns] = jnp.dot(
            edge_ref[:, :depths], weight, preferred_element_type=jnp.float32
        )


def last_project_kernel(first, edge_ref, left_ref, total_ref, *rest):
    shard_refs, (own_total_ref, their_total_ref) = rest[:-2], rest[-2:]
    block = own_total_ref.shape[0] // 2
    depth = sum(ref.shape[0] for ref in shard_refs)
    features = jnp.concatenate([left_ref[:, -depth:], edge_ref[:, -depth:]], axis=0)
    tile = 2 * HEAD
    for at in range(0, own_total_ref.shape[1], tile):
        here = slice(at, at + tile)
        columns = slice(first + at, first + at + tile)
        weight = jnp.concatenate([ref[:, columns] for ref in shard_refs], axis=0)
        total = total_ref[:, columns] + jnp.dot(
            features, weight, preferred_element_type=jnp.float32
        )
        own_total_ref[:block, here] = total[:block]
        own_total_ref[block:, here] = total[2 * block : 3 * block]
        their_total_ref[:block, here] = total[block : 2 * block].astype(jnp.bfloat16)
        their_total_ref[block:, here] = total[3 * block :].astype(jnp.bfloat16)


def add_kernel(total_ref, more_ref, out_ref):
    out_ref[...] = (total_ref[...] + more_ref[...]).astype(jnp.bfloat16)


def finish_kernel(total_ref, more_ref, ready_ref, out_ref, held, sems):
    block = out_ref.shape[0] // 2
    ctx = lax.axis_index("ctx")
    ready = ready_ref.shape[1]
    blocks = [(slice(0, block), ctx), (slice(block, 2 * block), 1 - ctx)]

    def copy(source_ref, which, first, sem):
        rows, place = blocks[which]
        there = pl.ds(pl.multiple_of(place * block, block), block)
        columns = pl.ds(first, source_ref.shape[1])
        return pltpu.make_async_copy(source_ref.at[rows], out_ref.at[there, columns], sem)

    copies = [copy(ready_ref, which, 0, sems.at[which]) for which in range(2)]
    for one in copies:
        one.start()
    for which, (rows, _) in enumerate(blocks):
        held[rows] = (total_ref[rows] + more_ref[rows]).astype(jnp.bfloat16)
        copies.append(copy(held, which, ready, sems.at[2 + which]))
        copies[-1].start()
    for one in copies:
        one.wait()


SMEM = functools.partial(pl.BlockSpec, memory_space=pltpu.SMEM)
VMEM = functools.partial(pl.BlockSpec, memory_space=pltpu.VMEM)
HBM = functools.partial(pl.BlockSpec, memory_space=pltpu.HBM)


def after(value, *others):
    return lax.optimization_barrier((value, *others))[0]


def body_edge(projections, block_source, clip_ids, out_weight):
    local_rows, row_width = projections.shape
    block_rows = local_rows // 2
    heads = row_width // (3 * HEAD)
    features = heads * HEAD
    depth, width = out_weight.shape
    count = lax.axis_size("dp")
    bf16 = jnp.bfloat16

    def call(kernel, name, shape, in_specs, dtypes=None, scratch=(), out_spec=VMEM()):
        many = isinstance(shape, list)
        shapes = shape if many else [shape]
        dtypes = dtypes or [bf16] * len(shapes)
        shapes = [jax.ShapeDtypeStruct(*one) for one in zip(shapes, dtypes, strict=True)]
        return pl.pallas_call(
            kernel,
            out_shape=shapes if many else shapes[0],
            in_specs=in_specs,
            out_specs=[out_spec] * len(shapes) if many else out_spec,
            scratch_shapes=scratch,
            cost_estimate=pl.CostEstimate(flops=0, bytes_accessed=0, transcendentals=0),
            compiler_params=pltpu.CompilerParams(vmem_limit_bytes=8 * MIB),
            name=name,
        )

    def around(value, step):
        places = ring_order(count // 4)
        moves = [(here, places[(at + step) % len(places)]) for at, here in enumerate(places)]
        return lax.ppermute(
            value, "dp", [(4 * here + rest, 4 * there + rest) for here, there in moves for rest in range(4)]
        )

    def to_side(value):
        return partner(value, "dp", 1)

    def to_core(value):
        return partner(value, "dp", 0)

    own = pltpu.with_memory_space_constraint(
        projections.reshape(2, block_rows, row_width), pltpu.HBM
    )
    shards = {(0, False): [out_weight]}
    from_partner = pltpu.with_memory_space_constraint(to_core(own), pltpu.VMEM)
    ahead = around(out_weight, 1)
    across = to_side(out_weight)
    staged = call(
        stage_kernel,
        "stage",
        own.shape,
        [SMEM(), HBM()],
        scratch=[pltpu.SemaphoreType.DMA],
    )(block_source, own)
    part_heads = [heads * 8 // 16, heads * 8 // 16]
    rows, *packed = call(
        pack_kernel,
        "pack",
        [(2, block_rows, row_width)] + [(block_rows, 2 * HEAD * some) for some in part_heads],
        [SMEM(), VMEM(), VMEM()],
        scratch=[pltpu.SemaphoreType.DMA((2,))],
    )(block_source, staged, from_partner)
    halos = [lax.ppermute(part, "ctx", [(0, 1), (1, 0)]) for part in packed]

    def edge_rows(part, *before):
        some = part_heads[part]
        return call(
            functools.partial(edge_kernel, sum(part_heads[:part])),
            "edge_rows",
            [(block_rows, some * HEAD), (block_rows, some // 2 * HEAD)],
            [SMEM(), VMEM(), VMEM()],
        )(after(clip_ids, *before), rows, halos[part])

    back = around(after(out_weight, staged), -1)
    ahead = after(ahead, *packed)
    shards[1, False], shards[0, True] = [ahead], [across]
    across = to_side(after(ahead, across))
    second = around(ahead, 1)
    inner, inner_other = call(
        inner_kernel,
        "inner_rows",
        [(block_rows, features), (block_rows, features // 2)],
        [SMEM(), VMEM()],
    )(after(clip_ids, ahead), rows)
    theirs = [to_core(inner_other)]

    back = after(back, inner)
    shards[3, False] = [back]
    back_across = to_side(back)
    shards[1, True] = [across]
    early = list(shards)
    origins = [*early, (2, False), (3, True), (2, True)]
    inner_total, inner_left = call(
        functools.partial(inner_project_kernel, origins, len(early)),
        "inner_project",
        [(local_rows, width), (local_rows, (len(origins) - len(early)) * depth)],
        [VMEM()] * (2 + len(early)),
        dtypes=[jnp.float32, bf16],
        scratch=[pltpu.VMEM((local_rows, len(early) * depth), bf16)],
    )(inner, *theirs, *[shards[origin][0] for origin in early])
    edges, edge_others = zip(*[edge_rows(part) for part in range(len(part_heads))], strict=True)
    second = after(second, inner_total, edges[0])
    cut = depth // 8 * 5
    shards[2, False] = [second]
    shards[3, True] = [back_across]
    shards[2, True] = [around(after(across, edges[0])[:cut], 1), to_side(second[cut:])]
    theirs = [to_core(part) for part in edge_others]

    arranged = call(
        functools.partial(arrange_kernel, origins, len(edges)),
        "arrange",
        (local_rows, len(origins) * depth),
        [VMEM()] * (len(edges) + len(theirs)),
        scratch=[
            pltpu.VMEM((block_rows, features), bf16),
            pltpu.VMEM((block_rows, features // 2), bf16),
        ],
    )(*edges, *theirs)
    pieces = [piece for origin in origins[:-1] for piece in shards[origin]]
    total = call(
        edge_project_kernel,
        "edge_project",
        (2 * local_rows, width),
        [VMEM()] * (3 + len(pieces)),
        dtypes=[jnp.float32],
    )(arranged, inner_left, inner_total, *pieces)
    sums = []
    first = 0
    for columns in (width // 3 * 2, width // 3):
        own_total, their_total = call(
            functools.partial(last_project_kernel, first),
            "last_project",
            [(local_rows, columns)] * 2,
            [VMEM()] * (3 + len(shards[origins[-1]])),
            dtypes=[jnp.float32, bf16],
        )(arranged, inner_left, total, *shards[origins[-1]])
        sums.append((own_total, to_core(their_total)))
        first += columns
    ready = call(add_kernel, "add", sums[0][0].shape, [VMEM()] * 2)(*sums[0])
    return call(
        finish_kernel,
        "finish",
        (local_rows, width),
        [VMEM()] * 3,
        scratch=[pltpu.VMEM(sums[1][0].shape, bf16), pltpu.SemaphoreType.DMA((4,))],
        out_spec=HBM(),
    )(*sums[1], ready)


def body(projections, block_source, clip_ids, out_weight):
    heads = projections.shape[1] // (3 * HEAD)
    two_and_two = lax.axis_size("ctx") == 2 and block_source.shape[2] == 2
    whole_tiles = out_weight.shape[0] % HEAD == 0 and heads % 16 == 0
    if two_and_two and whole_tiles and lax.axis_size("dp") == 16:
        return body_edge(projections, block_source, clip_ids, out_weight)
    return body_general(projections, block_source, clip_ids, out_weight)


def solution(mesh):
    return jax.shard_map(
        body,
        mesh=mesh,
        in_specs=(P(("dp", "ctx"), None), P("dp", "ctx", None), P("dp", None), P("dp", None)),
        out_specs=P(("dp", "ctx"), None),
        check_vma=False,
    )
```

profile of v0, /device:TPU:0, one launch (start us, length us, event | category | flops | bytes accessed | tf_op | source)
XLA Modules:
  0.0 42.8 jit_solution(3833323107468207921)
XLA Ops:
  0.0 0.5 %collective-permute-start = (bf16[2,128,6144]{2,1,0:T(8,128)(2,1)}, bf16[2,128,6144]{2,1,0:T(8,128)(2,1)S(1)}, u32[]{:S(2)}, u32[]{:S(2)}) collective-permute-start(bf16[2,128,6144]{2,1,0:T(8,128)(2,1)} %bitcast.1), channel_id=1, source_target_pairs={{0,2},{2,0},{4,6},{6,4},{8,10},{10,8},{12,14},{14,12},{16,18},{18,... | collective-permute-start | bytes 9437192 | tf_op jit(solution)/shard_map/ppermute | solution.py:21
  0.5 3.6 %collective-permute-start.5 = (bf16[128,1536]{1,0:T(8,128)(2,1)}, bf16[128,1536]{1,0:T(8,128)(2,1)S(1)}, u32[]{:S(2)}, u32[]{:S(2)}) collective-permute-start(bf16[128,1536]{1,0:T(8,128)(2,1)} %rest_0_.3), channel_id=1, source_target_pairs={{0,16},{2,18},{4,20},{6,22},{16,24},{18,26},{20,28},{22,30},{24,8}... | collective-permute-start | bytes 1179656 | tf_op jit(solution)/shard_map/ppermute | solution.py:371
  4.0 1.5 %collective-permute-start.7 = (bf16[128,1536]{1,0:T(8,128)(2,1)}, bf16[128,1536]{1,0:T(8,128)(2,1)S(1)}, u32[]{:S(2)}, u32[]{:S(2)}) collective-permute-start(bf16[128,1536]{1,0:T(8,128)(2,1)} %rest_0_.3), channel_id=1, source_target_pairs={{0,4},{2,6},{4,0},{6,2},{8,12},{10,14},{12,8},{14,10},{16,20},{18,... | collective-permute-start | bytes 1179656 | tf_op jit(solution)/shard_map/ppermute | solution.py:21
  5.5 0.7 %copy-done.2 = s32[1,1,2]{2,1,0:T(1,128)S(1)} copy-done((s32[1,1,2]{2,1,0:T(1,128)S(1)}, s32[1,1,2]{2,1,0:T(1,128)}, u32[]{:S(2)}) %copy-start.2) | copy-done | bytes 32
  6.2 2.4 %stage.1.own_ref = bf16[2,128,6144]{2,1,0:T(8,128)(2,1)S(1)} custom-call(s32[1,1,2]{2,1,0:T(1,128)S(1)} %copy-done.2, bf16[2,128,6144]{2,1,0:T(8,128)(2,1)} %bitcast.2), custom_call_target="tpu_custom_call" | custom-call | tf_op jit(solution)/shard_map/stage/pallas_call | solution.py:388
  8.6 0.0 copy-start
  8.6 0.0 copy-start.1
  8.7 0.0 collective-permute-done.partner_ref
  8.7 0.9 %pack.1 = (bf16[2,128,6144]{2,1,0:T(8,128)(2,1)S(1)}, bf16[128,2048]{1,0:T(8,128)(2,1)S(1)}, bf16[128,2048]{1,0:T(8,128)(2,1)S(1)}) custom-call(s32[1,1,2]{2,1,0:T(1,128)S(1)} %copy-done.2, bf16[2,128,6144]{2,1,0:T(8,128)(2,1)S(1)} %stage.1.own_ref, bf16[2,128,6144]{2,1,0:T(8,128)(2,1)S(1)} %collective-permute-done.partner_ref), custom_call_target="tpu_custom_call" | custom-call | tf_op jit(solution)/shard_map/pack/pallas_call | solution.py:396
  9.6 1.6 %collective-permute-start.1 = (bf16[128,2048]{1,0:T(8,128)(2,1)S(1)}, bf16[128,2048]{1,0:T(8,128)(2,1)S(1)}, u32[]{:S(2)}, u32[]{:S(2)}) collective-permute-start(bf16[128,2048]{1,0:T(8,128)(2,1)S(1)} %get-tuple-element.28), channel_id=1, source_target_pairs={{0,1},{1,0},{2,3},{3,2},{4,5},{5,4},{6,7},{7,6},{8,9},{9,8},{10,11... | collective-permute-start | bytes 1572872 | tf_op jit(solution)/shard_map/ppermute | solution.py:403
  11.2 0.0 copy-done
  11.2 0.2 collective-permute-start.8
  11.4 0.5 %collective-permute-start.2 = (bf16[128,2048]{1,0:T(8,128)(2,1)S(1)}, bf16[128,2048]{1,0:T(8,128)(2,1)S(1)}, u32[]{:S(2)}, u32[]{:S(2)}) collective-permute-start(bf16[128,2048]{1,0:T(8,128)(2,1)S(1)} %get-tuple-element.30), channel_id=1, source_target_pairs={{0,1},{1,0},{2,3},{3,2},{4,5},{5,4},{6,7},{7,6},{8,9},{9,8},{10,11... | collective-permute-start | bytes 1572872 | tf_op jit(solution)/shard_map/ppermute | solution.py:403
  11.9 1.9 %collective-permute-done.5.rest_1_ = bf16[128,1536]{1,0:T(8,128)(2,1)S(1)} collective-permute-done((bf16[128,1536]{1,0:T(8,128)(2,1)}, bf16[128,1536]{1,0:T(8,128)(2,1)S(1)}, u32[]{:S(2)}, u32[]{:S(2)}) %collective-permute-start.5) | collective-permute-done | bytes 393248 | tf_op jit(solution)/shard_map/ppermute | solution.py:371
  13.8 1.7 %collective-permute-done.7.rest_2_ = bf16[128,1536]{1,0:T(8,128)(2,1)S(1)} collective-permute-done((bf16[128,1536]{1,0:T(8,128)(2,1)}, bf16[128,1536]{1,0:T(8,128)(2,1)S(1)}, u32[]{:S(2)}, u32[]{:S(2)}) %collective-permute-start.7) | collective-permute-done | bytes 393248 | tf_op jit(solution)/shard_map/ppermute | solution.py:21
  15.5 1.5 %collective-permute-start.9 = (bf16[128,1536]{1,0:T(8,128)(2,1)S(1)}, bf16[128,1536]{1,0:T(8,128)(2,1)S(1)}, u32[]{:S(2)}, u32[]{:S(2)}) collective-permute-start(bf16[128,1536]{1,0:T(8,128)(2,1)S(1)} %collective-permute-done.5.rest_1_), channel_id=1, source_target_pairs={{0,4},{2,6},{4,0},{6,2},{8,12},{10,14},{12,8},{14,10},{16,20},{18,... | collective-permute-start | bytes 1179656 | tf_op jit(solution)/shard_map/ppermute | solution.py:21
  17.0 1.6 %collective-permute-start.10 = (bf16[128,1536]{1,0:T(8,128)(2,1)S(1)}, bf16[128,1536]{1,0:T(8,128)(2,1)S(1)}, u32[]{:S(2)}, u32[]{:S(2)}) collective-permute-start(bf16[128,1536]{1,0:T(8,128)(2,1)S(1)} %collective-permute-done.5.rest_1_), channel_id=1, source_target_pairs={{0,16},{2,18},{4,20},{6,22},{16,24},{18,26},{20,28},{22,30},{24,8}... | collective-permute-start | bytes 1179656 | tf_op jit(solution)/shard_map/ppermute | solution.py:371
  18.6 2.3 %inner_rows.1 = (bf16[128,2048]{1,0:T(8,128)(2,1)S(1)}, bf16[128,1024]{1,0:T(8,128)(2,1)S(1)}) custom-call(s32[1,4]{1,0:T(1,128)S(1)} %copy-done.1, bf16[2,128,6144]{2,1,0:T(8,128)(2,1)S(1)} %get-tuple-element.27.rows_ref), custom_call_target="tpu_custom_call" | custom-call | tf_op jit(solution)/shard_map/inner_rows/pallas_call | solution.py:419
  20.8 3.4 %collective-permute-done.8.rest_3_ = bf16[128,1536]{1,0:T(8,128)(2,1)S(1)} collective-permute-done((bf16[128,1536]{1,0:T(8,128)(2,1)S(1)}, bf16[128,1536]{1,0:T(8,128)(2,1)S(1)}, u32[]{:S(2)}, u32[]{:S(2)}) %collective-permute-start.8) | collective-permute-done | bytes 393248 | tf_op jit(solution)/shard_map/ppermute | solution.py:371
  24.3 0.0 collective-permute-start.6
  24.3 0.1 collective-permute-done.1.halo_ref
  24.4 1.0 %collective-permute-start.11 = (bf16[128,1536]{1,0:T(8,128)(2,1)S(1)}, bf16[128,1536]{1,0:T(8,128)(2,1)S(1)}, u32[]{:S(2)}, u32[]{:S(2)}) collective-permute-start(bf16[128,1536]{1,0:T(8,128)(2,1)S(1)} %collective-permute-done.8.rest_3_), channel_id=1, source_target_pairs={{0,4},{2,6},{4,0},{6,2},{8,12},{10,14},{12,8},{14,10},{16,20},{18,... | collective-permute-start | bytes 1179656 | tf_op jit(solution)/shard_map/ppermute | solution.py:21
  25.5 1.5 %edge_rows.2 = (bf16[128,1024]{1,0:T(8,128)(2,1)S(1)}, bf16[128,512]{1,0:T(8,128)(2,1)S(1)}) custom-call(s32[1,4]{1,0:T(1,128)S(1)} %copy-done.1, bf16[2,128,6144]{2,1,0:T(8,128)(2,1)S(1)} %get-tuple-element.27.rows_ref, bf16[128,2048]{1,0:T(8,128)(2,1)S(1)} %collective-permute-done.1.halo_ref), custom_call_target="tpu_custom_call" | custom-call | tf_op jit(solution)/shard_map/edge_rows/pallas_call | solution.py:407
  26.9 0.0 collective-permute-done.9.rest_4_
  27.0 1.7 %collective-permute-start.12 = (bf16[80,1536]{1,0:T(8,128)(2,1)S(1)}, bf16[80,1536]{1,0:T(8,128)(2,1)S(1)}, u32[]{:S(2)}, u32[]{:S(2)}) collective-permute-start(bf16[80,1536]{1,0:T(8,128)(2,1)S(1)} %slice.6), channel_id=1, source_target_pairs={{0,16},{2,18},{4,20},{6,22},{16,24},{18,26},{20,28},{22,30},{24,8}... | collective-permute-start | bytes 737288 | tf_op jit(solution)/shard_map/ppermute | solution.py:371
  28.7 0.0 collective-permute-done.6.their_ref
  28.7 0.9 %inner_project.1 = (f32[256,1536]{1,0:T(8,128)S(1)}, bf16[256,384]{1,0:T(8,128)(2,1)S(1)}) custom-call(bf16[128,2048]{1,0:T(8,128)(2,1)S(1)} %get-tuple-element.36.inner_ref, bf16[128,1024]{1,0:T(8,128)(2,1)S(1)} %collective-permute-done.6.their_ref, bf16[128,1536]{1,0:T(8,128)(2,1)S(1)} %copy-done, bf16[128,1536]{1,0:T(8,128)(2,1)S(1)} %collective-permute-done.5.rest_1_, ...), custom_call_target="tpu_custom_call" | custom-call | tf_op jit(solution)/shard_map/inner_project/pallas_call | solution.py:433
  29.6 2.5 %collective-permute-done.10.rest_5_ = bf16[128,1536]{1,0:T(8,128)(2,1)S(1)} collective-permute-done((bf16[128,1536]{1,0:T(8,128)(2,1)S(1)}, bf16[128,1536]{1,0:T(8,128)(2,1)S(1)}, u32[]{:S(2)}, u32[]{:S(2)}) %collective-permute-start.10) | collective-permute-done | bytes 393248 | tf_op jit(solution)/shard_map/ppermute | solution.py:371
  32.1 1.6 %collective-permute-start.13 = (bf16[48,1536]{1,0:T(8,128)(2,1)S(1)}, bf16[48,1536]{1,0:T(8,128)(2,1)S(1)}, u32[]{:S(2)}, u32[]{:S(2)}) collective-permute-start(bf16[48,1536]{1,0:T(8,128)(2,1)S(1)} %slice.7), channel_id=1, source_target_pairs={{0,4},{2,6},{4,0},{6,2},{8,12},{10,14},{12,8},{14,10},{16,20},{18,... | collective-permute-start | bytes 442376 | tf_op jit(solution)/shard_map/ppermute | solution.py:21
  33.6 1.0 %collective-permute-done.2.halo_ref = bf16[128,2048]{1,0:T(8,128)(2,1)S(1)} collective-permute-done((bf16[128,2048]{1,0:T(8,128)(2,1)S(1)}, bf16[128,2048]{1,0:T(8,128)(2,1)S(1)}, u32[]{:S(2)}, u32[]{:S(2)}) %collective-permute-start.2) | collective-permute-done | bytes 524320 | tf_op jit(solution)/shard_map/ppermute | solution.py:403
  34.7 1.5 %edge_rows.3 = (bf16[128,1024]{1,0:T(8,128)(2,1)S(1)}, bf16[128,512]{1,0:T(8,128)(2,1)S(1)}) custom-call(s32[1,4]{1,0:T(1,128)S(1)} %copy-done.1, bf16[2,128,6144]{2,1,0:T(8,128)(2,1)S(1)} %get-tuple-element.27.rows_ref, bf16[128,2048]{1,0:T(8,128)(2,1)S(1)} %collective-permute-done.2.halo_ref), custom_call_target="tpu_custom_call" | custom-call | tf_op jit(solution)/shard_map/edge_rows/pallas_call | solution.py:407
  36.1 0.1 collective-permute-start.4
  36.2 0.5 %collective-permute-start.3 = (bf16[128,512]{1,0:T(8,128)(2,1)S(1)}, bf16[128,512]{1,0:T(8,128)(2,1)S(1)}, u32[]{:S(2)}, u32[]{:S(2)}) collective-permute-start(bf16[128,512]{1,0:T(8,128)(2,1)S(1)} %get-tuple-element.32), channel_id=1, source_target_pairs={{0,2},{2,0},{4,6},{6,4},{8,10},{10,8},{12,14},{14,12},{16,18},{18,... | collective-permute-start | bytes 393224 | tf_op jit(solution)/shard_map/ppermute | solution.py:21
  36.7 0.8 %collective-permute-done.4.refs_3_ = bf16[128,512]{1,0:T(8,128)(2,1)S(1)} collective-permute-done((bf16[128,512]{1,0:T(8,128)(2,1)S(1)}, bf16[128,512]{1,0:T(8,128)(2,1)S(1)}, u32[]{:S(2)}, u32[]{:S(2)}) %collective-permute-start.4) | collective-permute-done | bytes 131104 | tf_op jit(solution)/shard_map/ppermute | solution.py:21
  37.6 0.2 collective-permute-done.3.refs_2_
  37.7 0.2 arrange.1.edge_ref
  37.9 0.0 collective-permute-done.11.rest_6_
  37.9 1.2 %edge_project.1.total_ref = f32[512,1536]{1,0:T(8,128)S(1)} custom-call(bf16[256,1024]{1,0:T(8,128)(2,1)S(1)} %arrange.1.edge_ref, bf16[256,384]{1,0:T(8,128)(2,1)S(1)} %get-tuple-element.41.left_ref, f32[256,1536]{1,0:T(8,128)S(1)} %get-tuple-element.42.inner_total_ref, bf16[128,1536]{1,0:T(8,128)(2,1)S(1)} %copy-done, ...), custom_call_target="tpu_custom_call" | custom-call | tf_op jit(solution)/shard_map/edge_project/pallas_call | solution.py:460
  39.1 0.0 collective-permute-done.13.rest_1_
  39.1 0.0 collective-permute-done.12.rest_0_
  39.2 0.4 last_project.3
  39.6 0.4 collective-permute-start.15
  40.0 0.3 last_project.2
  40.3 0.2 collective-permute-start.14
  40.5 1.1 %collective-permute-done.15.more_ref = bf16[256,1024]{1,0:T(8,128)(2,1)S(1)} collective-permute-done((bf16[256,1024]{1,0:T(8,128)(2,1)S(1)}, bf16[256,1024]{1,0:T(8,128)(2,1)S(1)}, u32[]{:S(2)}, u32[]{:S(2)}) %collective-permute-start.15) | collective-permute-done | bytes 524320 | tf_op jit(solution)/shard_map/ppermute | solution.py:21
  41.6 0.1 add.1.ready_ref
  41.6 0.3 collective-permute-done.14.more_ref
  41.9 0.9 %finish.1 = bf16[256,1536]{1,0:T(8,128)(2,1)} custom-call(f32[256,512]{1,0:T(8,128)S(1)} %get-tuple-element.45.total_ref, bf16[256,512]{1,0:T(8,128)(2,1)S(1)} %collective-permute-done.14.more_ref, bf16[256,1024]{1,0:T(8,128)(2,1)S(1)} %add.1.ready_ref), custom_call_target="tpu_custom_call" | custom-call | tf_op jit(solution)/shard_map/finish/pallas_call | solution.py:480
  (4 shorter events, 0.0 us)
Async XLA Ops:
  0.0 8.7 %collective-permute-start = (bf16[2,128,6144]{2,1,0:T(8,128)(2,1)}, bf16[2,128,6144]{2,1,0:T(8,128)(2,1)S(1)}, u32[]{:S(2)}, u32[]{:S(2)}) collective-permute-start(bf16[2,128,6144]{2,1,0:T(8,128)(2,1)} %bitcast.1), channel_id=1, source_target_pairs={{0,2},{2,0},{4,6},{6,4},{8,10},{10,8},{12,14},{14,12},{16,18},{18,... | collective-permute-start | bytes 9437192 | tf_op jit(solution)/shard_map/ppermute | solution.py:21
  0.5 13.3 %collective-permute-start.5 = (bf16[128,1536]{1,0:T(8,128)(2,1)}, bf16[128,1536]{1,0:T(8,128)(2,1)S(1)}, u32[]{:S(2)}, u32[]{:S(2)}) collective-permute-start(bf16[128,1536]{1,0:T(8,128)(2,1)} %rest_0_.3), channel_id=1, source_target_pairs={{0,16},{2,18},{4,20},{6,22},{16,24},{18,26},{20,28},{22,30},{24,8}... | collective-permute-start | bytes 1179656 | tf_op jit(solution)/shard_map/ppermute | solution.py:371
  4.0 11.5 %collective-permute-start.7 = (bf16[128,1536]{1,0:T(8,128)(2,1)}, bf16[128,1536]{1,0:T(8,128)(2,1)S(1)}, u32[]{:S(2)}, u32[]{:S(2)}) collective-permute-start(bf16[128,1536]{1,0:T(8,128)(2,1)} %rest_0_.3), channel_id=1, source_target_pairs={{0,4},{2,6},{4,0},{6,2},{8,12},{10,14},{12,8},{14,10},{16,20},{18,... | collective-permute-start | bytes 1179656 | tf_op jit(solution)/shard_map/ppermute | solution.py:21
  5.5 0.7 %copy-start.2 = (s32[1,1,2]{2,1,0:T(1,128)S(1)}, s32[1,1,2]{2,1,0:T(1,128)}, u32[]{:S(2)}) copy-start(s32[1,1,2]{2,1,0:T(1,128)} %source_ref.3) | copy-start | bytes 28
  8.6 2.5 %copy-start = (bf16[128,1536]{1,0:T(8,128)(2,1)S(1)}, bf16[128,1536]{1,0:T(8,128)(2,1)}, u32[]{:S(2)}) copy-start(bf16[128,1536]{1,0:T(8,128)(2,1)} %rest_0_.3) | copy-start | bytes 1179652
  8.6 9.9 %copy-start.1 = (s32[1,4]{1,0:T(1,128)S(1)}, s32[1,4]{1,0:T(1,128)}, u32[]{:S(2)}) copy-start(s32[1,4]{1,0:T(1,128)} %clip_ref.2) | copy-start | bytes 52
  9.6 14.9 %collective-permute-start.1 = (bf16[128,2048]{1,0:T(8,128)(2,1)S(1)}, bf16[128,2048]{1,0:T(8,128)(2,1)S(1)}, u32[]{:S(2)}, u32[]{:S(2)}) collective-permute-start(bf16[128,2048]{1,0:T(8,128)(2,1)S(1)} %get-tuple-element.28), channel_id=1, source_target_pairs={{0,1},{1,0},{2,3},{3,2},{4,5},{5,4},{6,7},{7,6},{8,9},{9,8},{10,11... | collective-permute-start | bytes 1572872 | tf_op jit(solution)/shard_map/ppermute | solution.py:403
  11.2 13.1 %collective-permute-start.8 = (bf16[128,1536]{1,0:T(8,128)(2,1)S(1)}, bf16[128,1536]{1,0:T(8,128)(2,1)S(1)}, u32[]{:S(2)}, u32[]{:S(2)}) collective-permute-start(bf16[128,1536]{1,0:T(8,128)(2,1)S(1)} %copy-done), channel_id=1, source_target_pairs={{0,8},{2,10},{4,12},{6,14},{16,0},{18,2},{20,4},{22,6},{24,16},{26... | collective-permute-start | bytes 1179656 | tf_op jit(solution)/shard_map/ppermute | solution.py:371
  11.4 23.3 %collective-permute-start.2 = (bf16[128,2048]{1,0:T(8,128)(2,1)S(1)}, bf16[128,2048]{1,0:T(8,128)(2,1)S(1)}, u32[]{:S(2)}, u32[]{:S(2)}) collective-permute-start(bf16[128,2048]{1,0:T(8,128)(2,1)S(1)} %get-tuple-element.30), channel_id=1, source_target_pairs={{0,1},{1,0},{2,3},{3,2},{4,5},{5,4},{6,7},{7,6},{8,9},{9,8},{10,11... | collective-permute-start | bytes 1572872 | tf_op jit(solution)/shard_map/ppermute | solution.py:403
  15.5 11.4 %collective-permute-start.9 = (bf16[128,1536]{1,0:T(8,128)(2,1)S(1)}, bf16[128,1536]{1,0:T(8,128)(2,1)S(1)}, u32[]{:S(2)}, u32[]{:S(2)}) collective-permute-start(bf16[128,1536]{1,0:T(8,128)(2,1)S(1)} %collective-permute-done.5.rest_1_), channel_id=1, source_target_pairs={{0,4},{2,6},{4,0},{6,2},{8,12},{10,14},{12,8},{14,10},{16,20},{18,... | collective-permute-start | bytes 1179656 | tf_op jit(solution)/shard_map/ppermute | solution.py:21
  17.0 15.1 %collective-permute-start.10 = (bf16[128,1536]{1,0:T(8,128)(2,1)S(1)}, bf16[128,1536]{1,0:T(8,128)(2,1)S(1)}, u32[]{:S(2)}, u32[]{:S(2)}) collective-permute-start(bf16[128,1536]{1,0:T(8,128)(2,1)S(1)} %collective-permute-done.5.rest_1_), channel_id=1, source_target_pairs={{0,16},{2,18},{4,20},{6,22},{16,24},{18,26},{20,28},{22,30},{24,8}... | collective-permute-start | bytes 1179656 | tf_op jit(solution)/shard_map/ppermute | solution.py:371
  24.3 4.4 %collective-permute-start.6 = (bf16[128,1024]{1,0:T(8,128)(2,1)S(1)}, bf16[128,1024]{1,0:T(8,128)(2,1)S(1)}, u32[]{:S(2)}, u32[]{:S(2)}) collective-permute-start(bf16[128,1024]{1,0:T(8,128)(2,1)S(1)} %get-tuple-element.37), channel_id=1, source_target_pairs={{0,2},{2,0},{4,6},{6,4},{8,10},{10,8},{12,14},{14,12},{16,18},{18,... | collective-permute-start | bytes 786440 | tf_op jit(solution)/shard_map/ppermute | solution.py:21
  24.4 13.5 %collective-permute-start.11 = (bf16[128,1536]{1,0:T(8,128)(2,1)S(1)}, bf16[128,1536]{1,0:T(8,128)(2,1)S(1)}, u32[]{:S(2)}, u32[]{:S(2)}) collective-permute-start(bf16[128,1536]{1,0:T(8,128)(2,1)S(1)} %collective-permute-done.8.rest_3_), channel_id=1, source_target_pairs={{0,4},{2,6},{4,0},{6,2},{8,12},{10,14},{12,8},{14,10},{16,20},{18,... | collective-permute-start | bytes 1179656 | tf_op jit(solution)/shard_map/ppermute | solution.py:21
  27.0 12.2 %collective-permute-start.12 = (bf16[80,1536]{1,0:T(8,128)(2,1)S(1)}, bf16[80,1536]{1,0:T(8,128)(2,1)S(1)}, u32[]{:S(2)}, u32[]{:S(2)}) collective-permute-start(bf16[80,1536]{1,0:T(8,128)(2,1)S(1)} %slice.6), channel_id=1, source_target_pairs={{0,16},{2,18},{4,20},{6,22},{16,24},{18,26},{20,28},{22,30},{24,8}... | collective-permute-start | bytes 737288 | tf_op jit(solution)/shard_map/ppermute | solution.py:371
  32.1 7.1 %collective-permute-start.13 = (bf16[48,1536]{1,0:T(8,128)(2,1)S(1)}, bf16[48,1536]{1,0:T(8,128)(2,1)S(1)}, u32[]{:S(2)}, u32[]{:S(2)}) collective-permute-start(bf16[48,1536]{1,0:T(8,128)(2,1)S(1)} %slice.7), channel_id=1, source_target_pairs={{0,4},{2,6},{4,0},{6,2},{8,12},{10,14},{12,8},{14,10},{16,20},{18,... | collective-permute-start | bytes 442376 | tf_op jit(solution)/shard_map/ppermute | solution.py:21
  36.1 1.4 %collective-permute-start.4 = (bf16[128,512]{1,0:T(8,128)(2,1)S(1)}, bf16[128,512]{1,0:T(8,128)(2,1)S(1)}, u32[]{:S(2)}, u32[]{:S(2)}) collective-permute-start(bf16[128,512]{1,0:T(8,128)(2,1)S(1)} %get-tuple-element.33), channel_id=1, source_target_pairs={{0,2},{2,0},{4,6},{6,4},{8,10},{10,8},{12,14},{14,12},{16,18},{18,... | collective-permute-start | bytes 393224 | tf_op jit(solution)/shard_map/ppermute | solution.py:21
  36.2 1.5 %collective-permute-start.3 = (bf16[128,512]{1,0:T(8,128)(2,1)S(1)}, bf16[128,512]{1,0:T(8,128)(2,1)S(1)}, u32[]{:S(2)}, u32[]{:S(2)}) collective-permute-start(bf16[128,512]{1,0:T(8,128)(2,1)S(1)} %get-tuple-element.32), channel_id=1, source_target_pairs={{0,2},{2,0},{4,6},{6,4},{8,10},{10,8},{12,14},{14,12},{16,18},{18,... | collective-permute-start | bytes 393224 | tf_op jit(solution)/shard_map/ppermute | solution.py:21
  39.6 2.0 %collective-permute-start.15 = (bf16[256,1024]{1,0:T(8,128)(2,1)S(1)}, bf16[256,1024]{1,0:T(8,128)(2,1)S(1)}, u32[]{:S(2)}, u32[]{:S(2)}) collective-permute-start(bf16[256,1024]{1,0:T(8,128)(2,1)S(1)} %get-tuple-element.48), channel_id=1, source_target_pairs={{0,2},{2,0},{4,6},{6,4},{8,10},{10,8},{12,14},{14,12},{16,18},{18,... | collective-permute-start | bytes 1572872 | tf_op jit(solution)/shard_map/ppermute | solution.py:21
  40.3 1.7 %collective-permute-start.14 = (bf16[256,512]{1,0:T(8,128)(2,1)S(1)}, bf16[256,512]{1,0:T(8,128)(2,1)S(1)}, u32[]{:S(2)}, u32[]{:S(2)}) collective-permute-start(bf16[256,512]{1,0:T(8,128)(2,1)S(1)} %get-tuple-element.46), channel_id=1, source_target_pairs={{0,2},{2,0},{4,6},{6,4},{8,10},{10,8},{12,14},{14,12},{16,18},{18,... | collective-permute-start | bytes 786440 | tf_op jit(solution)/shard_map/ppermute | solution.py:21
where the time goes:
time: 43 us; the launch traced here: 42.8 us
  starting transfers between devices  16.4 us (38%)
  waiting for transfers between devices  13.1 us (30%)
  Pallas kernels  12.5 us (29%)
  local copies, waits for them, and re-layouts  0.7 us (2%)
    ppermute x4, waiting for transfers between devices, around(): lax.ppermute(value, 'dp', [(4 * here + rest, 4 * there + rest) for here,...  7.81 us
    ppermute x10, starting transfers between devices, partner(): return lax.ppermute(value, axis, pairs)  7.22 us
    ppermute x4, starting transfers between devices, around(): lax.ppermute(value, 'dp', [(4 * here + rest, 4 * there + rest) for here,...  7.11 us
    ppermute x10, waiting for transfers between devices, partner(): return lax.ppermute(value, axis, pairs)  4.09 us
    pallas_call x2, Pallas kernels, edge_rows(): call(functools.partial(edge_kernel, sum(part_heads[:part])), 'edge_rows',...  2.94 us
    pallas_call x1, Pallas kernels, body_edge(): call(stage_kernel, 'stage', own.shape, [SMEM(), HBM()], scratch=[pltpu.Se...  2.44 us
    pallas_call x1, Pallas kernels, body_edge(): call(inner_kernel, 'inner_rows', [(block_rows, features), (block_rows, fe...  2.26 us
    ppermute x2, starting transfers between devices, body_edge(): halos = [lax.ppermute(part, 'ctx', [(0, 1), (1, 0)]) for part in packed]  2.09 us
  transfers between devices with their start and end apart: 16, of which 10 were waited for; matrix products, arithmetic and copies ran while one was open for 0% of the time, Pallas kernels for 26%

commit v1 on v0

--- a/solution.py
+++ b/solution.py
@@ -92,14 +92,25 @@
     copy.wait()
 
 
-def pack_kernel(source_ref, own_ref, partner_ref, rows_ref, *rest):
-    halo_refs, sems = rest[:-1], rest[-1]
-    ctx, dp = lax.axis_index("ctx"), lax.axis_index("dp")
+def place(source_ref, own_ref, block):
     slots = own_ref.shape[0]
+    source = source_ref[0, 0, block]
+    return source // (2 * slots) != lax.axis_index("dp"), lax.rem(source, slots)
+
+
+def pack_first_kernel(source_ref, own_ref, partner_ref, halo_ref):
+    away, slot = place(source_ref, own_ref, 1 - lax.axis_index("ctx"))
+    for head in range(halo_ref.shape[1] // (2 * HEAD)):
+        columns = slice(head * 3 * HEAD + HEAD, (head + 1) * 3 * HEAD)
+        halo_ref[:, head * 2 * HEAD : (head + 1) * 2 * HEAD] = jnp.where(
+            away, partner_ref[slot, :, columns], own_ref[slot, :, columns]
+        )
+
+
+def pack_kernel(source_ref, own_ref, partner_ref, rows_ref, halo_ref, sems):
+    ctx = lax.axis_index("ctx")
     for which, block in ((1, 1 - ctx), (0, ctx)):
-        source = source_ref[0, 0, block]
-        slot = lax.rem(source, slots)
-        away = source // (2 * slots) != dp
+        away, slot = place(source_ref, own_ref, block)
 
         @pl.when(jnp.logical_not(away))
         def _():
@@ -110,11 +121,13 @@
             pltpu.make_async_copy(partner_ref.at[slot], rows_ref.at[which], sems.at[which]).start()
 
     pltpu.make_async_copy(own_ref.at[0], rows_ref.at[1], sems.at[1]).wait()
-    first = HEAD
-    for halo_ref in halo_refs:
-        for at in range(0, halo_ref.shape[1], 2 * HEAD):
-            halo_ref[:, at : at + 2 * HEAD] = rows_ref[1, :, first : first + 2 * HEAD]
-            first += 3 * HEAD
+    heads = halo_ref.shape[1] // (2 * HEAD)
+    skipped = rows_ref.shape[2] // (3 * HEAD) - heads
+    for head in range(heads):
+        first = (skipped + head) * 3 * HEAD + HEAD
+        halo_ref[:, head * 2 * HEAD : (head + 1) * 2 * HEAD] = rows_ref[
+            1, :, first : first + 2 * HEAD
+        ]
     pltpu.make_async_copy(own_ref.at[0], rows_ref.at[0], sems.at[0]).wait()
 
 
@@ -393,13 +406,20 @@
         scratch=[pltpu.SemaphoreType.DMA],
     )(block_source, own)
     part_heads = [heads * 8 // 16, heads * 8 // 16]
-    rows, *packed = call(
+    packed_first = call(
+        pack_first_kernel,
+        "pack_first",
+        (block_rows, 2 * HEAD * part_heads[0]),
+        [SMEM(), VMEM(), VMEM()],
+    )(block_source, staged, from_partner)
+    rows, packed_last = call(
         pack_kernel,
         "pack",
-        [(2, block_rows, row_width)] + [(block_rows, 2 * HEAD * some) for some in part_heads],
+        [(2, block_rows, row_width), (block_rows, 2 * HEAD * part_heads[1])],
         [SMEM(), VMEM(), VMEM()],
         scratch=[pltpu.SemaphoreType.DMA((2,))],
-    )(block_source, staged, from_partner)
+    )(block_source, staged, after(from_partner, packed_first))
+    packed = [packed_first, packed_last]
     halos = [lax.ppermute(part, "ctx", [(0, 1), (1, 0)]) for part in packed]
 
     def edge_rows(part, *before):
@@ -414,8 +434,8 @@
     back = around(after(out_weight, staged), -1)
     ahead = after(ahead, *packed)
     shards[1, False], shards[0, True] = [ahead], [across]
-    across = to_side(after(ahead, across))
-    second = around(ahead, 1)
+    second = around(after(ahead, across), 1)
+    across = to_side(ahead)
     inner, inner_other = call(
         inner_kernel,
         "inner_rows",

time: 43 us -> 42.7 us (level)
  waiting for transfers between devices: 13.1 us -> 10.6 us
  starting transfers between devices: 16.4 us -> 18 us
  Pallas kernels: 12.5 us -> 13.1 us
    ppermute x10, waiting for transfers between devices: 4.09 us -> 2.6 us  [partner(): return lax.ppermute(value, axis, pairs)]
    ppermute x4, starting transfers between devices: 7.11 us -> 8.32 us  [around(): lax.ppermute(value, 'dp', [(4 * here + rest, 4 * there + rest) for here,...]
    ppermute x4, waiting for transfers between devices: 7.81 us -> 7.11 us  [around(): lax.ppermute(value, 'dp', [(4 * here + rest, 4 * there + rest) for here,...]
    pallas_call x1 -> x2, Pallas kernels: 0.9 us -> 1.48 us  [the longest x1 0.86 us: body_edge(): call(pack_kernel, 'pack', [(2, block_rows, row_width), (block_rows, 2 * H...]
  transfers between devices with their start and end apart: 16 -> 16, of which waited for: 10 -> 10; matrix products, arithmetic and copies ran while one was open for 0% -> 0% of each run, Pallas kernels for 26% -> 28%
where the time goes in v1:
time: 42.7 us; the launch traced here: 42.6 us
  starting transfers between devices  18 us (42%)
  Pallas kernels  13.1 us (31%)
  waiting for transfers between devices  10.6 us (25%)
  local copies, waits for them, and re-layouts  0.7 us (2%)
    ppermute x4, starting transfers between devices, around(): lax.ppermute(value, 'dp', [(4 * here + rest, 4 * there + rest) for here,...  8.32 us
    ppermute x10, starting transfers between devices, partner(): return lax.ppermute(value, axis, pairs)  7.5 us
    ppermute x4, waiting for transfers between devices, around(): lax.ppermute(value, 'dp', [(4 * here + rest, 4 * there + rest) for here,...  7.11 us
    pallas_call x2, Pallas kernels, edge_rows(): call(functools.partial(edge_kernel, sum(part_heads[:part])), 'edge_rows',...  2.95 us
    ppermute x10, waiting for transfers between devices, partner(): return lax.ppermute(value, axis, pairs)  2.6 us
    pallas_call x1, Pallas kernels, body_edge(): call(stage_kernel, 'stage', own.shape, [SMEM(), HBM()], scratch=[pltpu.Se...  2.44 us
    pallas_call x1, Pallas kernels, body_edge(): call(inner_kernel, 'inner_rows', [(block_rows, features), (block_rows, fe...  2.25 us
    ppermute x2, starting transfers between devices, body_edge(): halos = [lax.ppermute(part, 'ctx', [(0, 1), (1, 0)]) for part in packed]  2.16 us
  transfers between devices with their start and end apart: 16, of which 10 were waited for; matrix products, arithmetic and copies ran while one was open for 0% of the time, Pallas kernels for 28%

profile of v1, /device:TPU:0, one launch (start us, length us, event | category | flops | bytes accessed | tf_op | source)
XLA Modules:
  0.0 42.6 jit_solution(2709741162687776886)
XLA Ops:
  0.0 0.5 %collective-permute-start = (bf16[2,128,6144]{2,1,0:T(8,128)(2,1)}, bf16[2,128,6144]{2,1,0:T(8,128)(2,1)S(1)}, u32[]{:S(2)}, u32[]{:S(2)}) collective-permute-start(bf16[2,128,6144]{2,1,0:T(8,128)(2,1)} %bitcast.1), channel_id=1, source_target_pairs={{0,2},{2,0},{4,6},{6,4},{8,10},{10,8},{12,14},{14,12},{16,18},{18,... | collective-permute-start | bytes 9437192 | tf_op jit(solution)/shard_map/ppermute | solution.py:21
  0.5 3.6 %collective-permute-start.5 = (bf16[128,1536]{1,0:T(8,128)(2,1)}, bf16[128,1536]{1,0:T(8,128)(2,1)S(1)}, u32[]{:S(2)}, u32[]{:S(2)}) collective-permute-start(bf16[128,1536]{1,0:T(8,128)(2,1)} %rest_0_.3), channel_id=1, source_target_pairs={{0,16},{2,18},{4,20},{6,22},{16,24},{18,26},{20,28},{22,30},{24,8}... | collective-permute-start | bytes 1179656 | tf_op jit(solution)/shard_map/ppermute | solution.py:384
  4.0 1.5 %collective-permute-start.7 = (bf16[128,1536]{1,0:T(8,128)(2,1)}, bf16[128,1536]{1,0:T(8,128)(2,1)S(1)}, u32[]{:S(2)}, u32[]{:S(2)}) collective-permute-start(bf16[128,1536]{1,0:T(8,128)(2,1)} %rest_0_.3), channel_id=1, source_target_pairs={{0,4},{2,6},{4,0},{6,2},{8,12},{10,14},{12,8},{14,10},{16,20},{18,... | collective-permute-start | bytes 1179656 | tf_op jit(solution)/shard_map/ppermute | solution.py:21
  5.5 0.7 %copy-done.1 = s32[1,1,2]{2,1,0:T(1,128)S(1)} copy-done((s32[1,1,2]{2,1,0:T(1,128)S(1)}, s32[1,1,2]{2,1,0:T(1,128)}, u32[]{:S(2)}) %copy-start.1) | copy-done | bytes 32
  6.2 2.4 %stage.1.own_ref = bf16[2,128,6144]{2,1,0:T(8,128)(2,1)S(1)} custom-call(s32[1,1,2]{2,1,0:T(1,128)S(1)} %copy-done.1, bf16[2,128,6144]{2,1,0:T(8,128)(2,1)} %bitcast.2), custom_call_target="tpu_custom_call" | custom-call | tf_op jit(solution)/shard_map/stage/pallas_call | solution.py:401
  8.6 0.0 copy-start
  8.6 0.0 collective-permute-done.partner_ref
  8.7 0.6 %pack_first.1 = bf16[128,2048]{1,0:T(8,128)(2,1)S(1)} custom-call(s32[1,1,2]{2,1,0:T(1,128)S(1)} %copy-done.1, bf16[2,128,6144]{2,1,0:T(8,128)(2,1)S(1)} %stage.1.own_ref, bf16[2,128,6144]{2,1,0:T(8,128)(2,1)S(1)} %collective-permute-done.partner_ref), custom_call_target="tpu_custom_call" | custom-call | tf_op jit(solution)/shard_map/pack_first/pallas_call | solution.py:409
  9.3 0.0 copy-start.2
  9.3 1.6 %collective-permute-start.1 = (bf16[128,2048]{1,0:T(8,128)(2,1)S(1)}, bf16[128,2048]{1,0:T(8,128)(2,1)S(1)}, u32[]{:S(2)}, u32[]{:S(2)}) collective-permute-start(bf16[128,2048]{1,0:T(8,128)(2,1)S(1)} %pack_first.1), channel_id=1, source_target_pairs={{0,1},{1,0},{2,3},{3,2},{4,5},{5,4},{6,7},{7,6},{8,9},{9,8},{10,11... | collective-permute-start | bytes 1572872 | tf_op jit(solution)/shard_map/ppermute | solution.py:423
  10.9 0.2 collective-permute-start.8
  11.1 0.9 %pack.1 = (bf16[2,128,6144]{2,1,0:T(8,128)(2,1)S(1)}, bf16[128,2048]{1,0:T(8,128)(2,1)S(1)}) custom-call(s32[1,1,2]{2,1,0:T(1,128)S(1)} %copy-done.1, bf16[2,128,6144]{2,1,0:T(8,128)(2,1)S(1)} %stage.1.own_ref, bf16[2,128,6144]{2,1,0:T(8,128)(2,1)S(1)} %collective-permute-done.partner_ref), custom_call_target="tpu_custom_call" | custom-call | tf_op jit(solution)/shard_map/pack/pallas_call | solution.py:415
  12.0 0.6 %collective-permute-start.2 = (bf16[128,2048]{1,0:T(8,128)(2,1)S(1)}, bf16[128,2048]{1,0:T(8,128)(2,1)S(1)}, u32[]{:S(2)}, u32[]{:S(2)}) collective-permute-start(bf16[128,2048]{1,0:T(8,128)(2,1)S(1)} %get-tuple-element.30), channel_id=1, source_target_pairs={{0,1},{1,0},{2,3},{3,2},{4,5},{5,4},{6,7},{7,6},{8,9},{9,8},{10,11... | collective-permute-start | bytes 1572872 | tf_op jit(solution)/shard_map/ppermute | solution.py:423
  12.6 1.2 %collective-permute-done.5.rest_1_ = bf16[128,1536]{1,0:T(8,128)(2,1)S(1)} collective-permute-done((bf16[128,1536]{1,0:T(8,128)(2,1)}, bf16[128,1536]{1,0:T(8,128)(2,1)S(1)}, u32[]{:S(2)}, u32[]{:S(2)}) %collective-permute-start.5) | collective-permute-done | bytes 393248 | tf_op jit(solution)/shard_map/ppermute | solution.py:384
  13.8 1.5 %collective-permute-start.9 = (bf16[128,1536]{1,0:T(8,128)(2,1)S(1)}, bf16[128,1536]{1,0:T(8,128)(2,1)S(1)}, u32[]{:S(2)}, u32[]{:S(2)}) collective-permute-start(bf16[128,1536]{1,0:T(8,128)(2,1)S(1)} %collective-permute-done.5.rest_1_), channel_id=1, source_target_pairs={{0,4},{2,6},{4,0},{6,2},{8,12},{10,14},{12,8},{14,10},{16,20},{18,... | collective-permute-start | bytes 1179656 | tf_op jit(solution)/shard_map/ppermute | solution.py:21
  15.3 0.2 collective-permute-done.7.rest_2_
  15.5 3.1 %collective-permute-start.10 = (bf16[128,1536]{1,0:T(8,128)(2,1)S(1)}, bf16[128,1536]{1,0:T(8,128)(2,1)S(1)}, u32[]{:S(2)}, u32[]{:S(2)}) collective-permute-start(bf16[128,1536]{1,0:T(8,128)(2,1)S(1)} %collective-permute-done.5.rest_1_), channel_id=1, source_target_pairs={{0,16},{2,18},{4,20},{6,22},{16,24},{18,26},{20,28},{22,30},{24,8}... | collective-permute-start | bytes 1179656 | tf_op jit(solution)/shard_map/ppermute | solution.py:384
  18.6 2.3 %inner_rows.1 = (bf16[128,2048]{1,0:T(8,128)(2,1)S(1)}, bf16[128,1024]{1,0:T(8,128)(2,1)S(1)}) custom-call(s32[1,4]{1,0:T(1,128)S(1)} %copy-done.2, bf16[2,128,6144]{2,1,0:T(8,128)(2,1)S(1)} %get-tuple-element.28.rows_ref), custom_call_target="tpu_custom_call" | custom-call | tf_op jit(solution)/shard_map/inner_rows/pallas_call | solution.py:439
  20.8 3.1 %collective-permute-done.8.rest_3_ = bf16[128,1536]{1,0:T(8,128)(2,1)S(1)} collective-permute-done((bf16[128,1536]{1,0:T(8,128)(2,1)S(1)}, bf16[128,1536]{1,0:T(8,128)(2,1)S(1)}, u32[]{:S(2)}, u32[]{:S(2)}) %collective-permute-start.8) | collective-permute-done | bytes 393248 | tf_op jit(solution)/shard_map/ppermute | solution.py:384
  24.0 0.0 collective-permute-start.6
  24.0 0.2 collective-permute-done.1.halo_ref
  24.2 1.3 %collective-permute-start.11 = (bf16[128,1536]{1,0:T(8,128)(2,1)S(1)}, bf16[128,1536]{1,0:T(8,128)(2,1)S(1)}, u32[]{:S(2)}, u32[]{:S(2)}) collective-permute-start(bf16[128,1536]{1,0:T(8,128)(2,1)S(1)} %collective-permute-done.8.rest_3_), channel_id=1, source_target_pairs={{0,4},{2,6},{4,0},{6,2},{8,12},{10,14},{12,8},{14,10},{16,20},{18,... | collective-permute-start | bytes 1179656 | tf_op jit(solution)/shard_map/ppermute | solution.py:21
  25.5 1.5 %edge_rows.2 = (bf16[128,1024]{1,0:T(8,128)(2,1)S(1)}, bf16[128,512]{1,0:T(8,128)(2,1)S(1)}) custom-call(s32[1,4]{1,0:T(1,128)S(1)} %copy-done.2, bf16[2,128,6144]{2,1,0:T(8,128)(2,1)S(1)} %get-tuple-element.28.rows_ref, bf16[128,2048]{1,0:T(8,128)(2,1)S(1)} %collective-permute-done.1.halo_ref), custom_call_target="tpu_custom_call" | custom-call | tf_op jit(solution)/shard_map/edge_rows/pallas_call | solution.py:427
  27.0 0.0 collective-permute-done.9.rest_4_
  27.0 1.4 %collective-permute-start.12 = (bf16[80,1536]{1,0:T(8,128)(2,1)S(1)}, bf16[80,1536]{1,0:T(8,128)(2,1)S(1)}, u32[]{:S(2)}, u32[]{:S(2)}) collective-permute-start(bf16[80,1536]{1,0:T(8,128)(2,1)S(1)} %slice.6), channel_id=1, source_target_pairs={{0,16},{2,18},{4,20},{6,22},{16,24},{18,26},{20,28},{22,30},{24,8}... | collective-permute-start | bytes 737288 | tf_op jit(solution)/shard_map/ppermute | solution.py:384
  28.4 0.0 collective-permute-done.6.their_ref
  28.4 0.9 %inner_project.1 = (f32[256,1536]{1,0:T(8,128)S(1)}, bf16[256,384]{1,0:T(8,128)(2,1)S(1)}) custom-call(bf16[128,2048]{1,0:T(8,128)(2,1)S(1)} %get-tuple-element.36.inner_ref, bf16[128,1024]{1,0:T(8,128)(2,1)S(1)} %collective-permute-done.6.their_ref, bf16[128,1536]{1,0:T(8,128)(2,1)S(1)} %copy-done, bf16[128,1536]{1,0:T(8,128)(2,1)S(1)} %collective-permute-done.5.rest_1_, ...), custom_call_target="tpu_custom_call" | custom-call | tf_op jit(solution)/shard_map/inner_project/pallas_call | solution.py:453
  29.3 2.7 %collective-permute-done.10.rest_5_ = bf16[128,1536]{1,0:T(8,128)(2,1)S(1)} collective-permute-done((bf16[128,1536]{1,0:T(8,128)(2,1)S(1)}, bf16[128,1536]{1,0:T(8,128)(2,1)S(1)}, u32[]{:S(2)}, u32[]{:S(2)}) %collective-permute-start.10) | collective-permute-done | bytes 393248 | tf_op jit(solution)/shard_map/ppermute | solution.py:384
  32.1 1.6 %collective-permute-start.13 = (bf16[48,1536]{1,0:T(8,128)(2,1)S(1)}, bf16[48,1536]{1,0:T(8,128)(2,1)S(1)}, u32[]{:S(2)}, u32[]{:S(2)}) collective-permute-start(bf16[48,1536]{1,0:T(8,128)(2,1)S(1)} %slice.7), channel_id=1, source_target_pairs={{0,4},{2,6},{4,0},{6,2},{8,12},{10,14},{12,8},{14,10},{16,20},{18,... | collective-permute-start | bytes 442376 | tf_op jit(solution)/shard_map/ppermute | solution.py:21
  33.6 0.8 %collective-permute-done.2.halo_ref = bf16[128,2048]{1,0:T(8,128)(2,1)S(1)} collective-permute-done((bf16[128,2048]{1,0:T(8,128)(2,1)S(1)}, bf16[128,2048]{1,0:T(8,128)(2,1)S(1)}, u32[]{:S(2)}, u32[]{:S(2)}) %collective-permute-start.2) | collective-permute-done | bytes 524320 | tf_op jit(solution)/shard_map/ppermute | solution.py:423
  34.4 1.5 %edge_rows.3 = (bf16[128,1024]{1,0:T(8,128)(2,1)S(1)}, bf16[128,512]{1,0:T(8,128)(2,1)S(1)}) custom-call(s32[1,4]{1,0:T(1,128)S(1)} %copy-done.2, bf16[2,128,6144]{2,1,0:T(8,128)(2,1)S(1)} %get-tuple-element.28.rows_ref, bf16[128,2048]{1,0:T(8,128)(2,1)S(1)} %collective-permute-done.2.halo_ref), custom_call_target="tpu_custom_call" | custom-call | tf_op jit(solution)/shard_map/edge_rows/pallas_call | solution.py:427
  35.9 0.1 collective-permute-start.4
  35.9 0.5 %collective-permute-start.3 = (bf16[128,512]{1,0:T(8,128)(2,1)S(1)}, bf16[128,512]{1,0:T(8,128)(2,1)S(1)}, u32[]{:S(2)}, u32[]{:S(2)}) collective-permute-start(bf16[128,512]{1,0:T(8,128)(2,1)S(1)} %get-tuple-element.32), channel_id=1, source_target_pairs={{0,2},{2,0},{4,6},{6,4},{8,10},{10,8},{12,14},{14,12},{16,18},{18,... | collective-permute-start | bytes 393224 | tf_op jit(solution)/shard_map/ppermute | solution.py:21
  36.4 0.8 %collective-permute-done.4.refs_3_ = bf16[128,512]{1,0:T(8,128)(2,1)S(1)} collective-permute-done((bf16[128,512]{1,0:T(8,128)(2,1)S(1)}, bf16[128,512]{1,0:T(8,128)(2,1)S(1)}, u32[]{:S(2)}, u32[]{:S(2)}) %collective-permute-start.4) | collective-permute-done | bytes 131104 | tf_op jit(solution)/shard_map/ppermute | solution.py:21
  37.3 0.2 collective-permute-done.3.refs_2_
  37.5 0.2 arrange.1.edge_ref
  37.6 0.0 collective-permute-done.11.rest_6_
  37.7 1.2 %edge_project.1.total_ref = f32[512,1536]{1,0:T(8,128)S(1)} custom-call(bf16[256,1024]{1,0:T(8,128)(2,1)S(1)} %arrange.1.edge_ref, bf16[256,384]{1,0:T(8,128)(2,1)S(1)} %get-tuple-element.40.left_ref, f32[256,1536]{1,0:T(8,128)S(1)} %get-tuple-element.41.inner_total_ref, bf16[128,1536]{1,0:T(8,128)(2,1)S(1)} %copy-done, ...), custom_call_target="tpu_custom_call" | custom-call | tf_op jit(solution)/shard_map/edge_project/pallas_call | solution.py:480
  38.9 0.0 collective-permute-done.13.rest_1_
  38.9 0.0 collective-permute-done.12.rest_0_
  38.9 0.4 %last_project.3 = (f32[256,1024]{1,0:T(8,128)S(1)}, bf16[256,1024]{1,0:T(8,128)(2,1)S(1)}) custom-call(bf16[256,1024]{1,0:T(8,128)(2,1)S(1)} %arrange.1.edge_ref, bf16[256,384]{1,0:T(8,128)(2,1)S(1)} %get-tuple-element.40.left_ref, f32[512,1536]{1,0:T(8,128)S(1)} %edge_project.1.total_ref, bf16[80,1536]{1,0:T(8,128)(2,1)S(1)} %collective-permute-done.12.rest_0_, ...), custom_call_target="tpu_custom_call" | custom-call | tf_op jit(solution)/shard_map/last_project/pallas_call | solution.py:490
  39.3 0.4 collective-permute-start.15
  39.7 0.3 last_project.2
  40.0 0.3 collective-permute-start.14
  40.2 1.1 %collective-permute-done.15.more_ref = bf16[256,1024]{1,0:T(8,128)(2,1)S(1)} collective-permute-done((bf16[256,1024]{1,0:T(8,128)(2,1)S(1)}, bf16[256,1024]{1,0:T(8,128)(2,1)S(1)}, u32[]{:S(2)}, u32[]{:S(2)}) %collective-permute-start.15) | collective-permute-done | bytes 524320 | tf_op jit(solution)/shard_map/ppermute | solution.py:21
  41.3 0.1 add.1.ready_ref
  41.4 0.3 collective-permute-done.14.more_ref
  41.7 0.9 %finish.1 = bf16[256,1536]{1,0:T(8,128)(2,1)} custom-call(f32[256,512]{1,0:T(8,128)S(1)} %get-tuple-element.45.total_ref, bf16[256,512]{1,0:T(8,128)(2,1)S(1)} %collective-permute-done.14.more_ref, bf16[256,1024]{1,0:T(8,128)(2,1)S(1)} %add.1.ready_ref), custom_call_target="tpu_custom_call" | custom-call | tf_op jit(solution)/shard_map/finish/pallas_call | solution.py:500
  (5 shorter events, 0.0 us)
Async XLA Ops:
  0.0 8.6 %collective-permute-start = (bf16[2,128,6144]{2,1,0:T(8,128)(2,1)}, bf16[2,128,6144]{2,1,0:T(8,128)(2,1)S(1)}, u32[]{:S(2)}, u32[]{:S(2)}) collective-permute-start(bf16[2,128,6144]{2,1,0:T(8,128)(2,1)} %bitcast.1), channel_id=1, source_target_pairs={{0,2},{2,0},{4,6},{6,4},{8,10},{10,8},{12,14},{14,12},{16,18},{18,... | collective-permute-start | bytes 9437192 | tf_op jit(solution)/shard_map/ppermute | solution.py:21
  0.5 13.3 %collective-permute-start.5 = (bf16[128,1536]{1,0:T(8,128)(2,1)}, bf16[128,1536]{1,0:T(8,128)(2,1)S(1)}, u32[]{:S(2)}, u32[]{:S(2)}) collective-permute-start(bf16[128,1536]{1,0:T(8,128)(2,1)} %rest_0_.3), channel_id=1, source_target_pairs={{0,16},{2,18},{4,20},{6,22},{16,24},{18,26},{20,28},{22,30},{24,8}... | collective-permute-start | bytes 1179656 | tf_op jit(solution)/shard_map/ppermute | solution.py:384
  4.0 11.5 %collective-permute-start.7 = (bf16[128,1536]{1,0:T(8,128)(2,1)}, bf16[128,1536]{1,0:T(8,128)(2,1)S(1)}, u32[]{:S(2)}, u32[]{:S(2)}) collective-permute-start(bf16[128,1536]{1,0:T(8,128)(2,1)} %rest_0_.3), channel_id=1, source_target_pairs={{0,4},{2,6},{4,0},{6,2},{8,12},{10,14},{12,8},{14,10},{16,20},{18,... | collective-permute-start | bytes 1179656 | tf_op jit(solution)/shard_map/ppermute | solution.py:21
  5.5 0.7 %copy-start.1 = (s32[1,1,2]{2,1,0:T(1,128)S(1)}, s32[1,1,2]{2,1,0:T(1,128)}, u32[]{:S(2)}) copy-start(s32[1,1,2]{2,1,0:T(1,128)} %source_ref.5) | copy-start | bytes 28
  8.6 2.2 %copy-start = (bf16[128,1536]{1,0:T(8,128)(2,1)S(1)}, bf16[128,1536]{1,0:T(8,128)(2,1)}, u32[]{:S(2)}) copy-start(bf16[128,1536]{1,0:T(8,128)(2,1)} %rest_0_.3) | copy-start | bytes 1179652
  9.3 9.3 %copy-start.2 = (s32[1,4]{1,0:T(1,128)S(1)}, s32[1,4]{1,0:T(1,128)}, u32[]{:S(2)}) copy-start(s32[1,4]{1,0:T(1,128)} %clip_ref.2) | copy-start | bytes 52
  9.3 14.9 %collective-permute-start.1 = (bf16[128,2048]{1,0:T(8,128)(2,1)S(1)}, bf16[128,2048]{1,0:T(8,128)(2,1)S(1)}, u32[]{:S(2)}, u32[]{:S(2)}) collective-permute-start(bf16[128,2048]{1,0:T(8,128)(2,1)S(1)} %pack_first.1), channel_id=1, source_target_pairs={{0,1},{1,0},{2,3},{3,2},{4,5},{5,4},{6,7},{7,6},{8,9},{9,8},{10,11... | collective-permute-start | bytes 1572872 | tf_op jit(solution)/shard_map/ppermute | solution.py:423
  10.9 13.1 %collective-permute-start.8 = (bf16[128,1536]{1,0:T(8,128)(2,1)S(1)}, bf16[128,1536]{1,0:T(8,128)(2,1)S(1)}, u32[]{:S(2)}, u32[]{:S(2)}) collective-permute-start(bf16[128,1536]{1,0:T(8,128)(2,1)S(1)} %copy-done), channel_id=1, source_target_pairs={{0,8},{2,10},{4,12},{6,14},{16,0},{18,2},{20,4},{22,6},{24,16},{26... | collective-permute-start | bytes 1179656 | tf_op jit(solution)/shard_map/ppermute | solution.py:384
  12.0 22.4 %collective-permute-start.2 = (bf16[128,2048]{1,0:T(8,128)(2,1)S(1)}, bf16[128,2048]{1,0:T(8,128)(2,1)S(1)}, u32[]{:S(2)}, u32[]{:S(2)}) collective-permute-start(bf16[128,2048]{1,0:T(8,128)(2,1)S(1)} %get-tuple-element.30), channel_id=1, source_target_pairs={{0,1},{1,0},{2,3},{3,2},{4,5},{5,4},{6,7},{7,6},{8,9},{9,8},{10,11... | collective-permute-start | bytes 1572872 | tf_op jit(solution)/shard_map/ppermute | solution.py:423
  13.8 13.2 %collective-permute-start.9 = (bf16[128,1536]{1,0:T(8,128)(2,1)S(1)}, bf16[128,1536]{1,0:T(8,128)(2,1)S(1)}, u32[]{:S(2)}, u32[]{:S(2)}) collective-permute-start(bf16[128,1536]{1,0:T(8,128)(2,1)S(1)} %collective-permute-done.5.rest_1_), channel_id=1, source_target_pairs={{0,4},{2,6},{4,0},{6,2},{8,12},{10,14},{12,8},{14,10},{16,20},{18,... | collective-permute-start | bytes 1179656 | tf_op jit(solution)/shard_map/ppermute | solution.py:21
  15.5 16.5 %collective-permute-start.10 = (bf16[128,1536]{1,0:T(8,128)(2,1)S(1)}, bf16[128,1536]{1,0:T(8,128)(2,1)S(1)}, u32[]{:S(2)}, u32[]{:S(2)}) collective-permute-start(bf16[128,1536]{1,0:T(8,128)(2,1)S(1)} %collective-permute-done.5.rest_1_), channel_id=1, source_target_pairs={{0,16},{2,18},{4,20},{6,22},{16,24},{18,26},{20,28},{22,30},{24,8}... | collective-permute-start | bytes 1179656 | tf_op jit(solution)/shard_map/ppermute | solution.py:384
  24.0 4.5 %collective-permute-start.6 = (bf16[128,1024]{1,0:T(8,128)(2,1)S(1)}, bf16[128,1024]{1,0:T(8,128)(2,1)S(1)}, u32[]{:S(2)}, u32[]{:S(2)}) collective-permute-start(bf16[128,1024]{1,0:T(8,128)(2,1)S(1)} %get-tuple-element.37), channel_id=1, source_target_pairs={{0,2},{2,0},{4,6},{6,4},{8,10},{10,8},{12,14},{14,12},{16,18},{18,... | collective-permute-start | bytes 786440 | tf_op jit(solution)/shard_map/ppermute | solution.py:21
  24.2 13.5 %collective-permute-start.11 = (bf16[128,1536]{1,0:T(8,128)(2,1)S(1)}, bf16[128,1536]{1,0:T(8,128)(2,1)S(1)}, u32[]{:S(2)}, u32[]{:S(2)}) collective-permute-start(bf16[128,1536]{1,0:T(8,128)(2,1)S(1)} %collective-permute-done.8.rest_3_), channel_id=1, source_target_pairs={{0,4},{2,6},{4,0},{6,2},{8,12},{10,14},{12,8},{14,10},{16,20},{18,... | collective-permute-start | bytes 1179656 | tf_op jit(solution)/shard_map/ppermute | solution.py:21
  27.0 11.9 %collective-permute-start.12 = (bf16[80,1536]{1,0:T(8,128)(2,1)S(1)}, bf16[80,1536]{1,0:T(8,128)(2,1)S(1)}, u32[]{:S(2)}, u32[]{:S(2)}) collective-permute-start(bf16[80,1536]{1,0:T(8,128)(2,1)S(1)} %slice.6), channel_id=1, source_target_pairs={{0,16},{2,18},{4,20},{6,22},{16,24},{18,26},{20,28},{22,30},{24,8}... | collective-permute-start | bytes 737288 | tf_op jit(solution)/shard_map/ppermute | solution.py:384
  32.1 6.8 %collective-permute-start.13 = (bf16[48,1536]{1,0:T(8,128)(2,1)S(1)}, bf16[48,1536]{1,0:T(8,128)(2,1)S(1)}, u32[]{:S(2)}, u32[]{:S(2)}) collective-permute-start(bf16[48,1536]{1,0:T(8,128)(2,1)S(1)} %slice.7), channel_id=1, source_target_pairs={{0,4},{2,6},{4,0},{6,2},{8,12},{10,14},{12,8},{14,10},{16,20},{18,... | collective-permute-start | bytes 442376 | tf_op jit(solution)/shard_map/ppermute | solution.py:21
  35.9 1.4 %collective-permute-start.4 = (bf16[128,512]{1,0:T(8,128)(2,1)S(1)}, bf16[128,512]{1,0:T(8,128)(2,1)S(1)}, u32[]{:S(2)}, u32[]{:S(2)}) collective-permute-start(bf16[128,512]{1,0:T(8,128)(2,1)S(1)} %get-tuple-element.33), channel_id=1, source_target_pairs={{0,2},{2,0},{4,6},{6,4},{8,10},{10,8},{12,14},{14,12},{16,18},{18,... | collective-permute-start | bytes 393224 | tf_op jit(solution)/shard_map/ppermute | solution.py:21
  35.9 1.5 %collective-permute-start.3 = (bf16[128,512]{1,0:T(8,128)(2,1)S(1)}, bf16[128,512]{1,0:T(8,128)(2,1)S(1)}, u32[]{:S(2)}, u32[]{:S(2)}) collective-permute-start(bf16[128,512]{1,0:T(8,128)(2,1)S(1)} %get-tuple-element.32), channel_id=1, source_target_pairs={{0,2},{2,0},{4,6},{6,4},{8,10},{10,8},{12,14},{14,12},{16,18},{18,... | collective-permute-start | bytes 393224 | tf_op jit(solution)/shard_map/ppermute | solution.py:21
  39.3 2.0 %collective-permute-start.15 = (bf16[256,1024]{1,0:T(8,128)(2,1)S(1)}, bf16[256,1024]{1,0:T(8,128)(2,1)S(1)}, u32[]{:S(2)}, u32[]{:S(2)}) collective-permute-start(bf16[256,1024]{1,0:T(8,128)(2,1)S(1)} %get-tuple-element.48), channel_id=1, source_target_pairs={{0,2},{2,0},{4,6},{6,4},{8,10},{10,8},{12,14},{14,12},{16,18},{18,... | collective-permute-start | bytes 1572872 | tf_op jit(solution)/shard_map/ppermute | solution.py:21
  40.0 1.7 %collective-permute-start.14 = (bf16[256,512]{1,0:T(8,128)(2,1)S(1)}, bf16[256,512]{1,0:T(8,128)(2,1)S(1)}, u32[]{:S(2)}, u32[]{:S(2)}) collective-permute-start(bf16[256,512]{1,0:T(8,128)(2,1)S(1)} %get-tuple-element.46), channel_id=1, source_target_pairs={{0,2},{2,0},{4,6},{6,4},{8,10},{10,8},{12,14},{14,12},{16,18},{18,... | collective-permute-start | bytes 786440 | tf_op jit(solution)/shard_map/ppermute | solution.py:21

commit v2 on v1

--- a/solution.py
+++ b/solution.py
@@ -280,25 +280,31 @@
         out_ref[block:, at] = their_rows[:, there]
 
 
-def edge_project_kernel(edge_ref, left_ref, inner_total_ref, *rest):
+def add_products_kernel(left_ref, inner_total_ref, *rest):
     shard_refs, total_ref = rest[:-1], rest[-1]
-    rows = edge_ref.shape[0]
     depths = sum(ref.shape[0] for ref in shard_refs)
-    depth = edge_ref.shape[1] - depths
-    left = left_ref.shape[1] - depth
     tile = 2 * HEAD
     for first in range(0, total_ref.shape[1], tile):
         columns = slice(first, first + tile)
         weight = jnp.concatenate([ref[:, columns] for ref in shard_refs], axis=0)
-        total_ref[:rows, columns] = inner_total_ref[:, columns] + jnp.dot(
-            left_ref[:, :left], weight[-left:], preferred_element_type=jnp.float32
-        )
-        total_ref[rows:, columns] = jnp.dot(
+        total_ref[:, columns] = inner_total_ref[:, columns] + jnp.dot(
+            left_ref[:, :depths], weight, preferred_element_type=jnp.float32
+        )
+
+
+def edge_project_kernel(edge_ref, *rest):
+    shard_refs, total_ref = rest[:-1], rest[-1]
+    depths = sum(ref.shape[0] for ref in shard_refs)
+    tile = 2 * HEAD
+    for first in range(0, total_ref.shape[1], tile):
+        columns = slice(first, first + tile)
+        weight = jnp.concatenate([ref[:, columns] for ref in shard_refs], axis=0)
+        total_ref[:, columns] = jnp.dot(
             edge_ref[:, :depths], weight, preferred_element_type=jnp.float32
         )
 
 
-def last_project_kernel(first, edge_ref, left_ref, total_ref, *rest):
+def last_project_kernel(first, edge_ref, left_ref, inner_total_ref, edge_total_ref, *rest):
     shard_refs, (own_total_ref, their_total_ref) = rest[:-2], rest[-2:]
     block = own_total_ref.shape[0] // 2
     depth = sum(ref.shape[0] for ref in shard_refs)
@@ -308,13 +314,13 @@
         here = slice(at, at + tile)
         columns = slice(first + at, first + at + tile)
         weight = jnp.concatenate([ref[:, columns] for ref in shard_refs], axis=0)
-        total = total_ref[:, columns] + jnp.dot(
-            features, weight, preferred_element_type=jnp.float32
-        )
-        own_total_ref[:block, here] = total[:block]
-        own_total_ref[block:, here] = total[2 * block : 3 * block]
-        their_total_ref[:block, here] = total[block : 2 * block].astype(jnp.bfloat16)
-        their_total_ref[block:, here] = total[3 * block :].astype(jnp.bfloat16)
+        total = jnp.dot(features, weight, preferred_element_type=jnp.float32)
+        inner = inner_total_ref[:, columns] + total[: 2 * block]
+        edge = edge_total_ref[:, columns] + total[2 * block :]
+        own_total_ref[:block, here] = inner[:block]
+        own_total_ref[block:, here] = edge[:block]
+        their_total_ref[:block, here] = inner[block:].astype(jnp.bfloat16)
+        their_total_ref[block:, here] = edge[block:].astype(jnp.bfloat16)
 
 
 def add_kernel(total_ref, more_ref, out_ref):
@@ -466,6 +472,15 @@
     shards[2, True] = [around(after(across, edges[0])[:cut], 1), to_side(second[cut:])]
     theirs = [to_core(part) for part in edge_others]
 
+    more = [shards[origin][0] for origin in origins[len(early) : -1]]
+    inner_total = call(
+        add_products_kernel,
+        "add_products",
+        inner_total.shape,
+        [VMEM()] * (2 + len(more)),
+        dtypes=[jnp.float32],
+    )(inner_left, inner_total, *more)
+    theirs[-1] = after(theirs[-1], inner_total)
     arranged = call(
         functools.partial(arrange_kernel, origins, len(edges)),
         "arrange",
@@ -477,13 +492,13 @@
         ],
     )(*edges, *theirs)
     pieces = [piece for origin in origins[:-1] for piece in shards[origin]]
-    total = call(
+    edge_total = call(
         edge_project_kernel,
         "edge_project",
-        (2 * local_rows, width),
-        [VMEM()] * (3 + len(pieces)),
+        (local_rows, width),
+        [VMEM()] * (1 + len(pieces)),
         dtypes=[jnp.float32],
-    )(arranged, inner_left, inner_total, *pieces)
+    )(arranged, *pieces)
     sums = []
     first = 0
     for columns in (width // 3 * 2, width // 3):
@@ -491,9 +506,9 @@
             functools.partial(last_project_kernel, first),
             "last_project",
             [(local_rows, columns)] * 2,
-            [VMEM()] * (3 + len(shards[origins[-1]])),
+            [VMEM()] * (4 + len(shards[origins[-1]])),
             dtypes=[jnp.float32, bf16],
-        )(arranged, inner_left, total, *shards[origins[-1]])
+        )(arranged, inner_left, inner_total, edge_total, *shards[origins[-1]])
         sums.append((own_total, to_core(their_total)))
         first += columns
     ready = call(add_kernel, "add", sums[0][0].shape, [VMEM()] * 2)(*sums[0])

time: 42.7 us -> 42.5 us (level)
    pallas_call x1 -> x2, Pallas kernels: 1.18 us -> 1.36 us  [the longest x1 0.99 us: body_edge(): call(edge_project_kernel, 'edge_project', (local_rows, width), [VMEM()] *...]
where the time goes in v2:
time: 42.5 us; the launch traced here: 42.4 us
  starting transfers between devices  18 us (42%)
  Pallas kernels  13.2 us (31%)
  waiting for transfers between devices  10.3 us (24%)
  local copies, waits for them, and re-layouts  0.7 us (2%)
    ppermute x4, starting transfers between devices, around(): lax.ppermute(value, 'dp', [(4 * here + rest, 4 * there + rest) for here,...  8.32 us
    ppermute x10, starting transfers between devices, partner(): return lax.ppermute(value, axis, pairs)  7.52 us
    ppermute x4, waiting for transfers between devices, around(): lax.ppermute(value, 'dp', [(4 * here + rest, 4 * there + rest) for here,...  7.1 us
    pallas_call x2, Pallas kernels, edge_rows(): call(functools.partial(edge_kernel, sum(part_heads[:part])), 'edge_rows',...  2.94 us
    pallas_call x1, Pallas kernels, body_edge(): call(stage_kernel, 'stage', own.shape, [SMEM(), HBM()], scratch=[pltpu.Se...  2.44 us
    pallas_call x1, Pallas kernels, body_edge(): call(inner_kernel, 'inner_rows', [(block_rows, features), (block_rows, fe...  2.25 us
    ppermute x10, waiting for transfers between devices, partner(): return lax.ppermute(value, axis, pairs)  2.23 us
    ppermute x2, starting transfers between devices, body_edge(): halos = [lax.ppermute(part, 'ctx', [(0, 1), (1, 0)]) for part in packed]  2.16 us
  transfers between devices with their start and end apart: 16, of which 10 were waited for; matrix products, arithmetic and copies ran while one was open for 0% of the time, Pallas kernels for 28%

profile of v2, /device:TPU:0, one launch (start us, length us, event | category | flops | bytes accessed | tf_op | source)
XLA Modules:
  0.0 42.4 jit_solution(11946427873333521599)
XLA Ops:
  0.0 0.5 %collective-permute-start = (bf16[2,128,6144]{2,1,0:T(8,128)(2,1)}, bf16[2,128,6144]{2,1,0:T(8,128)(2,1)S(1)}, u32[]{:S(2)}, u32[]{:S(2)}) collective-permute-start(bf16[2,128,6144]{2,1,0:T(8,128)(2,1)} %bitcast.1), channel_id=1, source_target_pairs={{0,2},{2,0},{4,6},{6,4},{8,10},{10,8},{12,14},{14,12},{16,18},{18,... | collective-permute-start | bytes 9437192 | tf_op jit(solution)/shard_map/ppermute | solution.py:21
  0.5 3.6 %collective-permute-start.5 = (bf16[128,1536]{1,0:T(8,128)(2,1)}, bf16[128,1536]{1,0:T(8,128)(2,1)S(1)}, u32[]{:S(2)}, u32[]{:S(2)}) collective-permute-start(bf16[128,1536]{1,0:T(8,128)(2,1)} %rest_0_.3), channel_id=1, source_target_pairs={{0,16},{2,18},{4,20},{6,22},{16,24},{18,26},{20,28},{22,30},{24,8}... | collective-permute-start | bytes 1179656 | tf_op jit(solution)/shard_map/ppermute | solution.py:390
  4.0 1.5 %collective-permute-start.7 = (bf16[128,1536]{1,0:T(8,128)(2,1)}, bf16[128,1536]{1,0:T(8,128)(2,1)S(1)}, u32[]{:S(2)}, u32[]{:S(2)}) collective-permute-start(bf16[128,1536]{1,0:T(8,128)(2,1)} %rest_0_.3), channel_id=1, source_target_pairs={{0,4},{2,6},{4,0},{6,2},{8,12},{10,14},{12,8},{14,10},{16,20},{18,... | collective-permute-start | bytes 1179656 | tf_op jit(solution)/shard_map/ppermute | solution.py:21
  5.5 0.7 %copy-done.1 = s32[1,1,2]{2,1,0:T(1,128)S(1)} copy-done((s32[1,1,2]{2,1,0:T(1,128)S(1)}, s32[1,1,2]{2,1,0:T(1,128)}, u32[]{:S(2)}) %copy-start.1) | copy-done | bytes 32
  6.2 2.4 %stage.1.own_ref = bf16[2,128,6144]{2,1,0:T(8,128)(2,1)S(1)} custom-call(s32[1,1,2]{2,1,0:T(1,128)S(1)} %copy-done.1, bf16[2,128,6144]{2,1,0:T(8,128)(2,1)} %bitcast.2), custom_call_target="tpu_custom_call" | custom-call | tf_op jit(solution)/shard_map/stage/pallas_call | solution.py:407
  8.6 0.0 copy-start
  8.6 0.0 collective-permute-done.partner_ref
  8.7 0.6 %pack_first.1 = bf16[128,2048]{1,0:T(8,128)(2,1)S(1)} custom-call(s32[1,1,2]{2,1,0:T(1,128)S(1)} %copy-done.1, bf16[2,128,6144]{2,1,0:T(8,128)(2,1)S(1)} %stage.1.own_ref, bf16[2,128,6144]{2,1,0:T(8,128)(2,1)S(1)} %collective-permute-done.partner_ref), custom_call_target="tpu_custom_call" | custom-call | tf_op jit(solution)/shard_map/pack_first/pallas_call | solution.py:415
  9.3 0.0 copy-start.2
  9.3 1.6 %collective-permute-start.1 = (bf16[128,2048]{1,0:T(8,128)(2,1)S(1)}, bf16[128,2048]{1,0:T(8,128)(2,1)S(1)}, u32[]{:S(2)}, u32[]{:S(2)}) collective-permute-start(bf16[128,2048]{1,0:T(8,128)(2,1)S(1)} %pack_first.1), channel_id=1, source_target_pairs={{0,1},{1,0},{2,3},{3,2},{4,5},{5,4},{6,7},{7,6},{8,9},{9,8},{10,11... | collective-permute-start | bytes 1572872 | tf_op jit(solution)/shard_map/ppermute | solution.py:429
  10.9 0.2 collective-permute-start.8
  11.1 0.9 %pack.1 = (bf16[2,128,6144]{2,1,0:T(8,128)(2,1)S(1)}, bf16[128,2048]{1,0:T(8,128)(2,1)S(1)}) custom-call(s32[1,1,2]{2,1,0:T(1,128)S(1)} %copy-done.1, bf16[2,128,6144]{2,1,0:T(8,128)(2,1)S(1)} %stage.1.own_ref, bf16[2,128,6144]{2,1,0:T(8,128)(2,1)S(1)} %collective-permute-done.partner_ref), custom_call_target="tpu_custom_call" | custom-call | tf_op jit(solution)/shard_map/pack/pallas_call | solution.py:421
  12.0 0.6 %collective-permute-start.2 = (bf16[128,2048]{1,0:T(8,128)(2,1)S(1)}, bf16[128,2048]{1,0:T(8,128)(2,1)S(1)}, u32[]{:S(2)}, u32[]{:S(2)}) collective-permute-start(bf16[128,2048]{1,0:T(8,128)(2,1)S(1)} %get-tuple-element.31), channel_id=1, source_target_pairs={{0,1},{1,0},{2,3},{3,2},{4,5},{5,4},{6,7},{7,6},{8,9},{9,8},{10,11... | collective-permute-start | bytes 1572872 | tf_op jit(solution)/shard_map/ppermute | solution.py:429
  12.6 1.2 %collective-permute-done.5.rest_1_ = bf16[128,1536]{1,0:T(8,128)(2,1)S(1)} collective-permute-done((bf16[128,1536]{1,0:T(8,128)(2,1)}, bf16[128,1536]{1,0:T(8,128)(2,1)S(1)}, u32[]{:S(2)}, u32[]{:S(2)}) %collective-permute-start.5) | collective-permute-done | bytes 393248 | tf_op jit(solution)/shard_map/ppermute | solution.py:390
  13.8 1.5 %collective-permute-start.9 = (bf16[128,1536]{1,0:T(8,128)(2,1)S(1)}, bf16[128,1536]{1,0:T(8,128)(2,1)S(1)}, u32[]{:S(2)}, u32[]{:S(2)}) collective-permute-start(bf16[128,1536]{1,0:T(8,128)(2,1)S(1)} %collective-permute-done.5.rest_1_), channel_id=1, source_target_pairs={{0,4},{2,6},{4,0},{6,2},{8,12},{10,14},{12,8},{14,10},{16,20},{18,... | collective-permute-start | bytes 1179656 | tf_op jit(solution)/shard_map/ppermute | solution.py:21
  15.3 0.2 collective-permute-done.7.rest_2_
  15.5 3.1 %collective-permute-start.10 = (bf16[128,1536]{1,0:T(8,128)(2,1)S(1)}, bf16[128,1536]{1,0:T(8,128)(2,1)S(1)}, u32[]{:S(2)}, u32[]{:S(2)}) collective-permute-start(bf16[128,1536]{1,0:T(8,128)(2,1)S(1)} %collective-permute-done.5.rest_1_), channel_id=1, source_target_pairs={{0,16},{2,18},{4,20},{6,22},{16,24},{18,26},{20,28},{22,30},{24,8}... | collective-permute-start | bytes 1179656 | tf_op jit(solution)/shard_map/ppermute | solution.py:390
  18.6 2.3 %inner_rows.1 = (bf16[128,2048]{1,0:T(8,128)(2,1)S(1)}, bf16[128,1024]{1,0:T(8,128)(2,1)S(1)}) custom-call(s32[1,4]{1,0:T(1,128)S(1)} %copy-done.2, bf16[2,128,6144]{2,1,0:T(8,128)(2,1)S(1)} %get-tuple-element.29.rows_ref), custom_call_target="tpu_custom_call" | custom-call | tf_op jit(solution)/shard_map/inner_rows/pallas_call | solution.py:445
  20.8 3.1 %collective-permute-done.8.rest_3_ = bf16[128,1536]{1,0:T(8,128)(2,1)S(1)} collective-permute-done((bf16[128,1536]{1,0:T(8,128)(2,1)S(1)}, bf16[128,1536]{1,0:T(8,128)(2,1)S(1)}, u32[]{:S(2)}, u32[]{:S(2)}) %collective-permute-start.8) | collective-permute-done | bytes 393248 | tf_op jit(solution)/shard_map/ppermute | solution.py:390
  24.0 0.0 collective-permute-start.6
  24.0 0.2 collective-permute-done.1.halo_ref
  24.2 1.3 %collective-permute-start.11 = (bf16[128,1536]{1,0:T(8,128)(2,1)S(1)}, bf16[128,1536]{1,0:T(8,128)(2,1)S(1)}, u32[]{:S(2)}, u32[]{:S(2)}) collective-permute-start(bf16[128,1536]{1,0:T(8,128)(2,1)S(1)} %collective-permute-done.8.rest_3_), channel_id=1, source_target_pairs={{0,4},{2,6},{4,0},{6,2},{8,12},{10,14},{12,8},{14,10},{16,20},{18,... | collective-permute-start | bytes 1179656 | tf_op jit(solution)/shard_map/ppermute | solution.py:21
  25.5 1.5 %edge_rows.2 = (bf16[128,1024]{1,0:T(8,128)(2,1)S(1)}, bf16[128,512]{1,0:T(8,128)(2,1)S(1)}) custom-call(s32[1,4]{1,0:T(1,128)S(1)} %copy-done.2, bf16[2,128,6144]{2,1,0:T(8,128)(2,1)S(1)} %get-tuple-element.29.rows_ref, bf16[128,2048]{1,0:T(8,128)(2,1)S(1)} %collective-permute-done.1.halo_ref), custom_call_target="tpu_custom_call" | custom-call | tf_op jit(solution)/shard_map/edge_rows/pallas_call | solution.py:433
  27.0 0.0 collective-permute-done.9.rest_4_
  27.0 1.4 %collective-permute-start.12 = (bf16[80,1536]{1,0:T(8,128)(2,1)S(1)}, bf16[80,1536]{1,0:T(8,128)(2,1)S(1)}, u32[]{:S(2)}, u32[]{:S(2)}) collective-permute-start(bf16[80,1536]{1,0:T(8,128)(2,1)S(1)} %slice.6), channel_id=1, source_target_pairs={{0,16},{2,18},{4,20},{6,22},{16,24},{18,26},{20,28},{22,30},{24,8}... | collective-permute-start | bytes 737288 | tf_op jit(solution)/shard_map/ppermute | solution.py:390
  28.4 0.0 collective-permute-done.6.their_ref
  28.4 0.9 %inner_project.1 = (f32[256,1536]{1,0:T(8,128)S(1)}, bf16[256,384]{1,0:T(8,128)(2,1)S(1)}) custom-call(bf16[128,2048]{1,0:T(8,128)(2,1)S(1)} %get-tuple-element.37.inner_ref, bf16[128,1024]{1,0:T(8,128)(2,1)S(1)} %collective-permute-done.6.their_ref, bf16[128,1536]{1,0:T(8,128)(2,1)S(1)} %copy-done, bf16[128,1536]{1,0:T(8,128)(2,1)S(1)} %collective-permute-done.5.rest_1_, ...), custom_call_target="tpu_custom_call" | custom-call | tf_op jit(solution)/shard_map/inner_project/pallas_call | solution.py:459
  29.3 2.7 %collective-permute-done.10.rest_0_.rest_5_ = bf16[128,1536]{1,0:T(8,128)(2,1)S(1)} collective-permute-done((bf16[128,1536]{1,0:T(8,128)(2,1)S(1)}, bf16[128,1536]{1,0:T(8,128)(2,1)S(1)}, u32[]{:S(2)}, u32[]{:S(2)}) %collective-permute-start.10) | collective-permute-done | bytes 393248 | tf_op jit(solution)/shard_map/ppermute | solution.py:390
  32.1 1.6 %collective-permute-start.13 = (bf16[48,1536]{1,0:T(8,128)(2,1)S(1)}, bf16[48,1536]{1,0:T(8,128)(2,1)S(1)}, u32[]{:S(2)}, u32[]{:S(2)}) collective-permute-start(bf16[48,1536]{1,0:T(8,128)(2,1)S(1)} %slice.7), channel_id=1, source_target_pairs={{0,4},{2,6},{4,0},{6,2},{8,12},{10,14},{12,8},{14,10},{16,20},{18,... | collective-permute-start | bytes 442376 | tf_op jit(solution)/shard_map/ppermute | solution.py:21
  33.6 0.8 %collective-permute-done.2.halo_ref = bf16[128,2048]{1,0:T(8,128)(2,1)S(1)} collective-permute-done((bf16[128,2048]{1,0:T(8,128)(2,1)S(1)}, bf16[128,2048]{1,0:T(8,128)(2,1)S(1)}, u32[]{:S(2)}, u32[]{:S(2)}) %collective-permute-start.2) | collective-permute-done | bytes 524320 | tf_op jit(solution)/shard_map/ppermute | solution.py:429
  34.4 1.5 %edge_rows.3 = (bf16[128,1024]{1,0:T(8,128)(2,1)S(1)}, bf16[128,512]{1,0:T(8,128)(2,1)S(1)}) custom-call(s32[1,4]{1,0:T(1,128)S(1)} %copy-done.2, bf16[2,128,6144]{2,1,0:T(8,128)(2,1)S(1)} %get-tuple-element.29.rows_ref, bf16[128,2048]{1,0:T(8,128)(2,1)S(1)} %collective-permute-done.2.halo_ref), custom_call_target="tpu_custom_call" | custom-call | tf_op jit(solution)/shard_map/edge_rows/pallas_call | solution.py:433
  35.8 0.1 collective-permute-start.4
  35.9 0.5 %collective-permute-start.3 = (bf16[128,512]{1,0:T(8,128)(2,1)S(1)}, bf16[128,512]{1,0:T(8,128)(2,1)S(1)}, u32[]{:S(2)}, u32[]{:S(2)}) collective-permute-start(bf16[128,512]{1,0:T(8,128)(2,1)S(1)} %get-tuple-element.33), channel_id=1, source_target_pairs={{0,2},{2,0},{4,6},{6,4},{8,10},{10,8},{12,14},{14,12},{16,18},{18,... | collective-permute-start | bytes 393224 | tf_op jit(solution)/shard_map/ppermute | solution.py:21
  36.4 0.4 add_products.1.inner_total_ref
  36.8 0.5 %collective-permute-done.4.refs_3_ = bf16[128,512]{1,0:T(8,128)(2,1)S(1)} collective-permute-done((bf16[128,512]{1,0:T(8,128)(2,1)S(1)}, bf16[128,512]{1,0:T(8,128)(2,1)S(1)}, u32[]{:S(2)}, u32[]{:S(2)}) %collective-permute-start.4) | collective-permute-done | bytes 131104 | tf_op jit(solution)/shard_map/ppermute | solution.py:21
  37.3 0.2 collective-permute-done.3.refs_2_
  37.4 0.2 arrange.1.edge_ref
  37.6 1.0 %edge_project.1.edge_total_ref = f32[256,1536]{1,0:T(8,128)S(1)} custom-call(bf16[256,1024]{1,0:T(8,128)(2,1)S(1)} %arrange.1.edge_ref, bf16[128,1536]{1,0:T(8,128)(2,1)S(1)} %copy-done, bf16[128,1536]{1,0:T(8,128)(2,1)S(1)} %collective-permute-done.5.rest_1_, bf16[128,1536]{1,0:T(8,128)(2,1)S(1)} %collective-permute-done.7.rest_2_, ...), custom_call_target="tpu_custom_call" | custom-call | tf_op jit(solution)/shard_map/edge_project/pallas_call | solution.py:495
  38.6 0.0 collective-permute-done.13.rest_1_
  38.7 0.0 collective-permute-done.12.rest_0_
  38.7 0.4 last_project.3
  39.1 0.4 collective-permute-start.15
  39.5 0.3 last_project.2
  39.7 0.3 collective-permute-start.14
  40.0 1.1 %collective-permute-done.15.more_ref = bf16[256,1024]{1,0:T(8,128)(2,1)S(1)} collective-permute-done((bf16[256,1024]{1,0:T(8,128)(2,1)S(1)}, bf16[256,1024]{1,0:T(8,128)(2,1)S(1)}, u32[]{:S(2)}, u32[]{:S(2)}) %collective-permute-start.15) | collective-permute-done | bytes 524320 | tf_op jit(solution)/shard_map/ppermute | solution.py:21
  41.1 0.1 add.1.ready_ref
  41.2 0.3 collective-permute-done.14.more_ref
  41.4 0.9 %finish.1 = bf16[256,1536]{1,0:T(8,128)(2,1)} custom-call(f32[256,512]{1,0:T(8,128)S(1)} %get-tuple-element.47.total_ref, bf16[256,512]{1,0:T(8,128)(2,1)S(1)} %collective-permute-done.14.more_ref, bf16[256,1024]{1,0:T(8,128)(2,1)S(1)} %add.1.ready_ref), custom_call_target="tpu_custom_call" | custom-call | tf_op jit(solution)/shard_map/finish/pallas_call | solution.py:515
  (6 shorter events, 0.0 us)
Async XLA Ops:
  0.0 8.6 %collective-permute-start = (bf16[2,128,6144]{2,1,0:T(8,128)(2,1)}, bf16[2,128,6144]{2,1,0:T(8,128)(2,1)S(1)}, u32[]{:S(2)}, u32[]{:S(2)}) collective-permute-start(bf16[2,128,6144]{2,1,0:T(8,128)(2,1)} %bitcast.1), channel_id=1, source_target_pairs={{0,2},{2,0},{4,6},{6,4},{8,10},{10,8},{12,14},{14,12},{16,18},{18,... | collective-permute-start | bytes 9437192 | tf_op jit(solution)/shard_map/ppermute | solution.py:21
  0.5 13.3 %collective-permute-start.5 = (bf16[128,1536]{1,0:T(8,128)(2,1)}, bf16[128,1536]{1,0:T(8,128)(2,1)S(1)}, u32[]{:S(2)}, u32[]{:S(2)}) collective-permute-start(bf16[128,1536]{1,0:T(8,128)(2,1)} %rest_0_.3), channel_id=1, source_target_pairs={{0,16},{2,18},{4,20},{6,22},{16,24},{18,26},{20,28},{22,30},{24,8}... | collective-permute-start | bytes 1179656 | tf_op jit(solution)/shard_map/ppermute | solution.py:390
  4.0 11.5 %collective-permute-start.7 = (bf16[128,1536]{1,0:T(8,128)(2,1)}, bf16[128,1536]{1,0:T(8,128)(2,1)S(1)}, u32[]{:S(2)}, u32[]{:S(2)}) collective-permute-start(bf16[128,1536]{1,0:T(8,128)(2,1)} %rest_0_.3), channel_id=1, source_target_pairs={{0,4},{2,6},{4,0},{6,2},{8,12},{10,14},{12,8},{14,10},{16,20},{18,... | collective-permute-start | bytes 1179656 | tf_op jit(solution)/shard_map/ppermute | solution.py:21
  5.5 0.7 %copy-start.1 = (s32[1,1,2]{2,1,0:T(1,128)S(1)}, s32[1,1,2]{2,1,0:T(1,128)}, u32[]{:S(2)}) copy-start(s32[1,1,2]{2,1,0:T(1,128)} %source_ref.5) | copy-start | bytes 28
  8.6 2.2 %copy-start = (bf16[128,1536]{1,0:T(8,128)(2,1)S(1)}, bf16[128,1536]{1,0:T(8,128)(2,1)}, u32[]{:S(2)}) copy-start(bf16[128,1536]{1,0:T(8,128)(2,1)} %rest_0_.3) | copy-start | bytes 1179652
  9.3 9.3 %copy-start.2 = (s32[1,4]{1,0:T(1,128)S(1)}, s32[1,4]{1,0:T(1,128)}, u32[]{:S(2)}) copy-start(s32[1,4]{1,0:T(1,128)} %clip_ref.2) | copy-start | bytes 52
  9.3 14.9 %collective-permute-start.1 = (bf16[128,2048]{1,0:T(8,128)(2,1)S(1)}, bf16[128,2048]{1,0:T(8,128)(2,1)S(1)}, u32[]{:S(2)}, u32[]{:S(2)}) collective-permute-start(bf16[128,2048]{1,0:T(8,128)(2,1)S(1)} %pack_first.1), channel_id=1, source_target_pairs={{0,1},{1,0},{2,3},{3,2},{4,5},{5,4},{6,7},{7,6},{8,9},{9,8},{10,11... | collective-permute-start | bytes 1572872 | tf_op jit(solution)/shard_map/ppermute | solution.py:429
  10.9 13.1 %collective-permute-start.8 = (bf16[128,1536]{1,0:T(8,128)(2,1)S(1)}, bf16[128,1536]{1,0:T(8,128)(2,1)S(1)}, u32[]{:S(2)}, u32[]{:S(2)}) collective-permute-start(bf16[128,1536]{1,0:T(8,128)(2,1)S(1)} %copy-done), channel_id=1, source_target_pairs={{0,8},{2,10},{4,12},{6,14},{16,0},{18,2},{20,4},{22,6},{24,16},{26... | collective-permute-start | bytes 1179656 | tf_op jit(solution)/shard_map/ppermute | solution.py:390
  12.0 22.4 %collective-permute-start.2 = (bf16[128,2048]{1,0:T(8,128)(2,1)S(1)}, bf16[128,2048]{1,0:T(8,128)(2,1)S(1)}, u32[]{:S(2)}, u32[]{:S(2)}) collective-permute-start(bf16[128,2048]{1,0:T(8,128)(2,1)S(1)} %get-tuple-element.31), channel_id=1, source_target_pairs={{0,1},{1,0},{2,3},{3,2},{4,5},{5,4},{6,7},{7,6},{8,9},{9,8},{10,11... | collective-permute-start | bytes 1572872 | tf_op jit(solution)/shard_map/ppermute | solution.py:429
  13.8 13.2 %collective-permute-start.9 = (bf16[128,1536]{1,0:T(8,128)(2,1)S(1)}, bf16[128,1536]{1,0:T(8,128)(2,1)S(1)}, u32[]{:S(2)}, u32[]{:S(2)}) collective-permute-start(bf16[128,1536]{1,0:T(8,128)(2,1)S(1)} %collective-permute-done.5.rest_1_), channel_id=1, source_target_pairs={{0,4},{2,6},{4,0},{6,2},{8,12},{10,14},{12,8},{14,10},{16,20},{18,... | collective-permute-start | bytes 1179656 | tf_op jit(solution)/shard_map/ppermute | solution.py:21
  15.5 16.5 %collective-permute-start.10 = (bf16[128,1536]{1,0:T(8,128)(2,1)S(1)}, bf16[128,1536]{1,0:T(8,128)(2,1)S(1)}, u32[]{:S(2)}, u32[]{:S(2)}) collective-permute-start(bf16[128,1536]{1,0:T(8,128)(2,1)S(1)} %collective-permute-done.5.rest_1_), channel_id=1, source_target_pairs={{0,16},{2,18},{4,20},{6,22},{16,24},{18,26},{20,28},{22,30},{24,8}... | collective-permute-start | bytes 1179656 | tf_op jit(solution)/shard_map/ppermute | solution.py:390
  24.0 4.5 %collective-permute-start.6 = (bf16[128,1024]{1,0:T(8,128)(2,1)S(1)}, bf16[128,1024]{1,0:T(8,128)(2,1)S(1)}, u32[]{:S(2)}, u32[]{:S(2)}) collective-permute-start(bf16[128,1024]{1,0:T(8,128)(2,1)S(1)} %get-tuple-element.38), channel_id=1, source_target_pairs={{0,2},{2,0},{4,6},{6,4},{8,10},{10,8},{12,14},{14,12},{16,18},{18,... | collective-permute-start | bytes 786440 | tf_op jit(solution)/shard_map/ppermute | solution.py:21
  24.2 12.3 %collective-permute-start.11 = (bf16[128,1536]{1,0:T(8,128)(2,1)S(1)}, bf16[128,1536]{1,0:T(8,128)(2,1)S(1)}, u32[]{:S(2)}, u32[]{:S(2)}) collective-permute-start(bf16[128,1536]{1,0:T(8,128)(2,1)S(1)} %collective-permute-done.8.rest_3_), channel_id=1, source_target_pairs={{0,4},{2,6},{4,0},{6,2},{8,12},{10,14},{12,8},{14,10},{16,20},{18,... | collective-permute-start | bytes 1179656 | tf_op jit(solution)/shard_map/ppermute | solution.py:21
  27.0 11.7 %collective-permute-start.12 = (bf16[80,1536]{1,0:T(8,128)(2,1)S(1)}, bf16[80,1536]{1,0:T(8,128)(2,1)S(1)}, u32[]{:S(2)}, u32[]{:S(2)}) collective-permute-start(bf16[80,1536]{1,0:T(8,128)(2,1)S(1)} %slice.6), channel_id=1, source_target_pairs={{0,16},{2,18},{4,20},{6,22},{16,24},{18,26},{20,28},{22,30},{24,8}... | collective-permute-start | bytes 737288 | tf_op jit(solution)/shard_map/ppermute | solution.py:390
  32.1 6.6 %collective-permute-start.13 = (bf16[48,1536]{1,0:T(8,128)(2,1)S(1)}, bf16[48,1536]{1,0:T(8,128)(2,1)S(1)}, u32[]{:S(2)}, u32[]{:S(2)}) collective-permute-start(bf16[48,1536]{1,0:T(8,128)(2,1)S(1)} %slice.7), channel_id=1, source_target_pairs={{0,4},{2,6},{4,0},{6,2},{8,12},{10,14},{12,8},{14,10},{16,20},{18,... | collective-permute-start | bytes 442376 | tf_op jit(solution)/shard_map/ppermute | solution.py:21
  35.8 1.4 %collective-permute-start.4 = (bf16[128,512]{1,0:T(8,128)(2,1)S(1)}, bf16[128,512]{1,0:T(8,128)(2,1)S(1)}, u32[]{:S(2)}, u32[]{:S(2)}) collective-permute-start(bf16[128,512]{1,0:T(8,128)(2,1)S(1)} %get-tuple-element.34), channel_id=1, source_target_pairs={{0,2},{2,0},{4,6},{6,4},{8,10},{10,8},{12,14},{14,12},{16,18},{18,... | collective-permute-start | bytes 393224 | tf_op jit(solution)/shard_map/ppermute | solution.py:21
  35.9 1.5 %collective-permute-start.3 = (bf16[128,512]{1,0:T(8,128)(2,1)S(1)}, bf16[128,512]{1,0:T(8,128)(2,1)S(1)}, u32[]{:S(2)}, u32[]{:S(2)}) collective-permute-start(bf16[128,512]{1,0:T(8,128)(2,1)S(1)} %get-tuple-element.33), channel_id=1, source_target_pairs={{0,2},{2,0},{4,6},{6,4},{8,10},{10,8},{12,14},{14,12},{16,18},{18,... | collective-permute-start | bytes 393224 | tf_op jit(solution)/shard_map/ppermute | solution.py:21
  39.1 2.0 %collective-permute-start.15 = (bf16[256,1024]{1,0:T(8,128)(2,1)S(1)}, bf16[256,1024]{1,0:T(8,128)(2,1)S(1)}, u32[]{:S(2)}, u32[]{:S(2)}) collective-permute-start(bf16[256,1024]{1,0:T(8,128)(2,1)S(1)} %get-tuple-element.50), channel_id=1, source_target_pairs={{0,2},{2,0},{4,6},{6,4},{8,10},{10,8},{12,14},{14,12},{16,18},{18,... | collective-permute-start | bytes 1572872 | tf_op jit(solution)/shard_map/ppermute | solution.py:21
  39.7 1.7 %collective-permute-start.14 = (bf16[256,512]{1,0:T(8,128)(2,1)S(1)}, bf16[256,512]{1,0:T(8,128)(2,1)S(1)}, u32[]{:S(2)}, u32[]{:S(2)}) collective-permute-start(bf16[256,512]{1,0:T(8,128)(2,1)S(1)} %get-tuple-element.48), channel_id=1, source_target_pairs={{0,2},{2,0},{4,6},{6,4},{8,10},{10,8},{12,14},{14,12},{16,18},{18,... | collective-permute-start | bytes 786440 | tf_op jit(solution)/shard_map/ppermute | solution.py:21
